TPU v7x, 128 devices: a whole 4x4x4 slice. The times are simulated.
128 devices in a mesh: seq: 64 (over z_lo, x, y, core), tp: 2 (over z_hi).
Axes of the slice: x: 4, y: 4, z: 4 (z_hi: 2, z_lo: 2; z = z_hi * 2 + z_lo), core: 2. Of those that a mesh axis runs over, the one named last changes fastest.
Arguments:
- hidden: bfloat16 [65536, 1408], P('seq'), may hold values from -8.5 to 8.5
- out_cotangent: bfloat16 [65536, 1408], P('seq'), may hold values from -6 to 6
- qkv_weight: bfloat16 [1408, 3, 1408], P(None, None, 'tp'), may hold values from -0.15625 to 0.15625
- out_weight: bfloat16 [1408, 1408], P('tp'), may hold values from -0.15625 to 0.15625
Outputs:
- grad_hidden: bfloat16 [65536, 1408], P('seq', 'tp')
- qkv_grad: float32 [1408, 3, 1408], P('seq', None, 'tp')
- out_grad: float32 [1408, 1408], P(('tp', 'seq'))
All inputs are finite; a program needn't handle non-finite values.
Results may differ from a plain program's by a relative error of at most 0.015.
The roundings to bfloat16 on the way count: a program that leaves them out, or rounds other values in their place, can miss the bound.
Values may be sent and summed in bfloat16 or wider, within the bound.
No kernel may reach another device: no remote copies, remote signals or barrier semaphores. Data moves between devices by JAX's collectives and lax.ppermute only.
A program may use at most 192 MiB of HBM per device.

v0:
```python
import jax
import jax.numpy as jnp
from jax import lax
from jax.sharding import PartitionSpec as P

HEAD_DIM = 88
P_SIZE = 256


def attend(stack):
    scale = stack.shape[-1] ** (-0.5)
    query = stack[:, :, 0]
    key = stack[:, :, 1]
    value = stack[:, :, 2]
    grad_attn = stack[:, :, 3]
    scores = jnp.einsum("iphe,jphe->phij", query, key, preferred_element_type=jnp.float32) * scale
    peak = jnp.max(scores, axis=-1, keepdims=True)
    expo = jnp.exp(scores - peak)
    prob = expo / jnp.sum(expo, axis=-1, keepdims=True)
    weights = prob.astype(jnp.bfloat16)
    attn = jnp.einsum("phij,jphe->iphe", weights, value, preferred_element_type=jnp.float32).astype(
        jnp.bfloat16
    )
    dweights = jnp.einsum("iphe,jphe->phij", grad_attn, value, preferred_element_type=jnp.float32)
    dscores = (prob * (dweights - jnp.sum(prob * dweights, axis=-1, keepdims=True)) * scale).astype(
        jnp.bfloat16
    )
    dvalue = jnp.einsum(
        "phij,iphe->jphe", weights, grad_attn, preferred_element_type=jnp.float32
    ).astype(jnp.bfloat16)
    dquery = jnp.einsum("phij,jphe->iphe", dscores, key, preferred_element_type=jnp.float32).astype(
        jnp.bfloat16
    )
    dkey = jnp.einsum("phij,iphe->jphe", dscores, query, preferred_element_type=jnp.float32).astype(
        jnp.bfloat16
    )
    return jnp.stack([attn, dquery, dkey, dvalue], axis=2)


def halve(partial_value):
    return lax.psum_scatter(partial_value, "tp", scatter_dimension=1, tiled=True)


def project(rows_in, rows_grad, weight_flat, out_weight):
    qkv = jnp.dot(rows_in, weight_flat, preferred_element_type=jnp.float32).astype(jnp.bfloat16)
    grad_attn = jnp.einsum(
        "td,cd->tc", rows_grad, out_weight, preferred_element_type=jnp.float32
    ).astype(jnp.bfloat16)
    return jnp.concatenate([qkv, grad_attn], axis=1)


def shards(hidden, out_cotangent, qkv_weight, out_weight):
    tokens_here, width = hidden.shape
    local_width = qkv_weight.shape[2]
    heads_here = local_width // HEAD_DIM
    frames_here = tokens_here // P_SIZE
    weight_flat = qkv_weight.reshape(width, 3 * local_width)
    stacked = project(hidden, out_cotangent, weight_flat, out_weight)
    stacked = stacked.reshape(frames_here, P_SIZE, 4, heads_here, HEAD_DIM)
    result = attend(lax.all_to_all(stacked, "seq", split_axis=1, concat_axis=0, tiled=True))
    returned = lax.all_to_all(result, "seq", split_axis=0, concat_axis=1, tiled=True)
    flat = returned.reshape(tokens_here, 4 * local_width)
    attn_rows = flat[:, :local_width]
    dqkv = flat[:, local_width:]
    partial_value = jnp.einsum("tk,fk->tf", dqkv, weight_flat, preferred_element_type=jnp.float32)
    grad_hidden = halve(partial_value).astype(jnp.bfloat16)
    n_seq = lax.axis_size("seq")
    qkv_rows = width // n_seq
    columns = hidden
    qkv_grad = lax.psum_scatter(
        jnp.einsum("tc,tf->cf", columns, dqkv, preferred_element_type=jnp.float32),
        "seq",
        scatter_dimension=0,
        tiled=True,
    ).reshape(qkv_rows, 3, local_width)
    columns = attn_rows
    out_grad = lax.psum_scatter(
        jnp.einsum("tc,td->cd", columns, out_cotangent, preferred_element_type=jnp.float32),
        "seq",
        scatter_dimension=0,
        tiled=True,
    )
    return (grad_hidden, qkv_grad, out_grad)


def solution(mesh):
    return jax.shard_map(
        shards,
        mesh=mesh,
        in_specs=(P("seq", None), P("seq", None), P(None, None, "tp"), P("tp", None)),
        out_specs=(P("seq", "tp"), P("seq", None, "tp"), P(("tp", "seq"), None)),
        check_vma=False,
    )
```

profile of v0, /device:TPU:32, one launch (start us, length us, event | category | flops | bytes accessed | tf_op | source)
XLA Modules:
  0.0 1025.5 jit_solution(17963007867673034122)
XLA Ops:
  8.1 1.8 copy-done
  9.8 9.2 convolution_convert_fusion
  19.0 2.4 convolution_convert_fusion.1
  21.4 3.1 pad_maximum_fusion
  24.6 10.5 %reshape.23 = bf16[4,256,4,8,88]{1,0,4,3,2:T(4,128)(2,1)} reshape(bf16[1024,2816]{0,1:T(8,128)(2,1)} %pad_maximum_fusion) | data formatting | bytes 11534336 | tf_op jit(solution)/shard_map/reshape | solution.py:59
  35.1 15.3 %copy.26 = bf16[4,256,4,8,88]{4,3,2,0,1:T(8,128)(2,1)} copy(bf16[4,256,4,8,88]{1,0,4,3,2:T(4,128)(2,1)} %reshape.23) | data formatting | bytes 11534336 | tf_op jit(solution)/shard_map/reshape | solution.py:59
  50.4 105.6 %all_to_all.33 = bf16[4,256,4,8,88]{4,3,2,0,1:T(8,128)(2,1)} all-to-all(bf16[4,256,4,8,88]{4,3,2,0,1:T(8,128)(2,1)} %copy.26), channel_id=1, replica_groups=mesh['seq'=64,'tp'=2] {'seq'}, dimensions={1} | all-to-all | bytes 11534336 | tf_op jit(solution)/shard_map/all_to_all | solution.py:60
  156.0 9.2 copy.28
  165.2 6.4 fusion.64
  171.6 4.2 copy.50
  175.8 4.2 copy.51
  180.0 3.1 fusion.53
  183.1 4.4 fusion.66
  187.5 4.2 copy.49
  191.6 4.3 copy.52
  196.0 6.3 fusion.50
  202.3 14.8 %fusion.46 = bf16[256,4,1,8,88]{0,4,3,1,2:T(8,128)(2,1)} fusion(f32[4,8,256,256]{2,3,1,0:T(8,128)} %fusion.50, bf16[256,4,1,8,88]{0,4,3,1,2:T(8,128)(2,1)} %copy.51, f32[4,8,256,256]{2,3,1,0:T(8,128)} %get-tuple-element.19, f32[4,8,256]{2,1,0:T(8,128)S(1)} %get-tuple-element.18), kind=kOutput, calls=%fused_computation.33 | convolution fusion | flops 384508160 | bytes 19693568 | tf_op jit(solution)/shard_map/phij,jphe->iphe/dot_general | solution.py:31
  217.1 14.8 %fusion.43 = bf16[256,4,1,8,88]{0,4,3,1,2:T(8,128)(2,1)} fusion(f32[4,8,256,256]{2,3,1,0:T(8,128)} %fusion.50, bf16[256,4,1,8,88]{0,4,3,1,2:T(8,128)(2,1)} %copy.50, f32[4,8,256,256]{2,3,1,0:T(8,128)} %get-tuple-element.19, f32[4,8,256]{2,1,0:T(8,128)S(1)} %get-tuple-element.18), kind=kOutput, calls=%fused_computation.32 | convolution fusion | flops 384508160 | bytes 19693568 | tf_op jit(solution)/shard_map/phij,iphe->jphe/dot_general | solution.py:34
  231.9 4.7 fusion.40
  236.6 5.0 fusion.37
  241.6 3.6 pad_maximum_fusion.1
  245.2 14.1 %copy.37 = bf16[256,4,4,8,88]{4,3,1,2,0:T(8,128)(2,1)} copy(bf16[256,4,4,8,88]{0,4,3,1,2:T(8,128)(2,1)} %pad_maximum_fusion.1) | data formatting | bytes 11534336 | tf_op jit(solution)/shard_map/stack | solution.py:37
  259.3 103.4 %all_to_all.34 = bf16[256,4,4,8,88]{4,3,1,2,0:T(8,128)(2,1)} all-to-all(bf16[256,4,4,8,88]{4,3,1,2,0:T(8,128)(2,1)} %copy.37), channel_id=1, replica_groups=mesh['seq'=64,'tp'=2] {'seq'}, dimensions={0} | all-to-all | bytes 11534336 | tf_op jit(solution)/shard_map/all_to_all | solution.py:61
  362.7 9.0 copy.39
  371.7 15.6 %reshape.24 = bf16[1024,2816]{1,0:T(8,128)(2,1)} reshape(bf16[4,64,4,4,8,88]{5,4,3,2,1,0:T(8,128)(2,1)} %copy.39) | data formatting | bytes 11534336 | tf_op jit(solution)/shard_map/reshape | solution.py:62
  387.4 12.8 %fusion.17 = f32[1024,1408]{0,1:T(8,128)} fusion(bf16[1408,2112]{0,1:T(8,128)(2,1)} %bitcast.68, bf16[1024,2816]{1,0:T(8,128)(2,1)} %reshape.24), kind=kOutput, calls=%fused_computation.17 | convolution fusion | flops 6090129408 | bytes 16171008 | tf_op jit(solution)/shard_map/tk,fk->tf/dot_general | solution.py:65
  400.2 0.0 all-reduce.5.cloned.1.call-start
  400.2 15.5 %convolution_bitcast_fusion = f32[1408,2112]{0,1:T(8,128)} fusion(bf16[1024,1408]{1,0:T(8,128)(2,1)S(1)} %copy-done, bf16[1024,2816]{1,0:T(8,128)(2,1)} %reshape.24), kind=kOutput, calls=%fused_computation.2 | convolution fusion | flops 6090129408 | bytes 19234816 | tf_op jit(solution)/shard_map/tc,tf->cf/dot_general | solution.py:71
  415.8 6.6 fusion.35
  422.4 170.0 %fusion = f32[16,1408]{1,0:T(8,128)S(1)} fusion(f32[704,1408]{1,0:T(8,128)} %fusion.35), kind=kCustom, calls=%all-reduce-scatter | all-reduce-scatter fusion | flops 1441793 | bytes 4055552
  592.4 1.9 collective-permute-start
  594.3 1.9 collective-permute-start.1
  596.2 1.9 collective-permute-start.10
  598.2 1.9 collective-permute-start.11
  600.1 1.9 collective-permute-start.19
  602.0 9.9 collective-permute-done.19
  612.0 1.9 collective-permute-start.12
  613.9 1.9 collective-permute-start.13
  615.9 1.9 collective-permute-start.14
  617.8 1.9 collective-permute-start.15
  619.7 1.9 collective-permute-start.16
  621.7 1.9 collective-permute-start.17
  623.6 1.6 collective-permute-done.13
  625.2 2.7 collective-permute-start.18
  627.9 0.1 collective-permute-done.14
  628.0 2.0 collective-permute-start.2
  630.1 0.6 collective-permute-done.15
  630.7 13.1 %collective-permute-start.3 = (f32[16,1408]{1,0:T(8,128)S(1)}, f32[16,1408]{1,0:T(8,128)S(1)}, u32[]{:S(2)}, u32[]{:S(2)}) collective-permute-start(f32[16,1408]{1,0:T(8,128)S(1)} %fusion), channel_id=1, source_target_pairs={{0,8},{2,10},{4,12},{6,14},{8,16},{10,18},{12,20},{14,22},{16,24},... | collective-permute-start | bytes 270344
  643.8 1.9 collective-permute-start.4
  645.8 1.9 collective-permute-start.5
  647.7 1.9 collective-permute-start.6
  649.7 1.9 collective-permute-start.7
  651.6 1.9 collective-permute-start.8
  653.6 1.9 collective-permute-start.9
  655.6 0.7 fusion.65
  657.7 3.4 collective-permute-done.7
  661.1 3.3 collective-permute-done.8
  664.4 2.6 collective-permute-done.9
  667.0 32.3 %concatenate.4 = f32[331,1408]{1,0:T(8,128)} concatenate(f32[11,1408]{1,0:T(8,128)S(1)} %collective-permute-done.19, f32[16,1408]{1,0:T(8,128)} %copy-done.10, f32[16,1408]{1,0:T(8,128)} %copy-done.9, f32[16,1408]{1,0:T(8,128)} %copy-done.8, f32[16,1408]{1,0:T(8,128)} %copy-done.7, f32[16,1408]{1,0:T(8,128)} %copy-done.6, f32[16,1408]{1,0:T(8,128)} %copy-done.5, ...), dimensions={0} | concatenate | bytes 3728384
  699.3 1.6 constant_dynamic-slice_fusion
  700.9 3.2 convert_element_type.51
  704.0 308.5 %all-reduce.5.cloned.1.call-done = f32[1408,2112]{0,1:T(8,128)} async-done(((f32[1408,2112]{0,1:T(8,128)}), f32[1408,2112]{0,1:T(8,128)}) %all-reduce.5.cloned.1.call-update) | async-done | bytes 11894800
  1012.5 3.0 constant_dynamic-slice_fusion.1
  1015.5 2.3 copy.40
  (49 shorter events, 0.2 us)
Async XLA Ops:
  8.0 1.8 copy-start
  8.0 692.9 %reduce-scatter.5.cloned.1.call-start = ((), (), s32[]{:S(2)}) async-start(), calls=%async_computation.3 | async-start | bytes 8650752 | tf_op jit(solution)/shard_map/reduce_scatter | solution.py:41
  9.8 9.2 copy-start.2
  9.8 9.2 copy-start.15
  231.9 4.7 copy-start.1
  236.6 5.0 copy-start.3
  236.6 5.0 copy-start.4
  400.2 612.4 %all-reduce.5.cloned.1.call-start = ((), (), s32[]{:S(2)}) async-start(), calls=%async_computation.4 | async-start | bytes 23789568
  415.8 239.8 %copy-start.14 = (u32[128]{0:T(128)S(1)}, u32[128]{0:T(128)}, u32[]{:S(2)}) copy-start(u32[128]{0:T(128)} %constant.8) | copy-start | bytes 1540
  592.4 21.5 %collective-permute-start = (f32[16,1408]{1,0:T(8,128)S(1)}, f32[16,1408]{1,0:T(8,128)S(1)}, u32[]{:S(2)}, u32[]{:S(2)}) collective-permute-start(f32[16,1408]{1,0:T(8,128)S(1)} %fusion), channel_id=1, source_target_pairs={{0,2},{2,4},{4,6},{6,8},{8,10},{10,12},{12,14},{14,16},{16,18},{18... | collective-permute-start | bytes 270344
  594.3 21.5 %collective-permute-start.1 = (f32[16,1408]{1,0:T(8,128)S(1)}, f32[16,1408]{1,0:T(8,128)S(1)}, u32[]{:S(2)}, u32[]{:S(2)}) collective-permute-start(f32[16,1408]{1,0:T(8,128)S(1)} %fusion), channel_id=1, source_target_pairs={{0,4},{2,6},{4,8},{6,10},{8,12},{10,14},{12,16},{14,18},{16,20},{1... | collective-permute-start | bytes 270344
  596.2 21.5 %collective-permute-start.10 = (f32[16,1408]{1,0:T(8,128)S(1)}, f32[16,1408]{1,0:T(8,128)S(1)}, u32[]{:S(2)}, u32[]{:S(2)}) collective-permute-start(f32[16,1408]{1,0:T(8,128)S(1)} %fusion), channel_id=1, source_target_pairs={{0,22},{2,24},{4,26},{6,28},{8,30},{10,32},{12,34},{14,36},{16,38}... | collective-permute-start | bytes 270344
  598.2 21.6 %collective-permute-start.11 = (f32[16,1408]{1,0:T(8,128)S(1)}, f32[16,1408]{1,0:T(8,128)S(1)}, u32[]{:S(2)}, u32[]{:S(2)}) collective-permute-start(f32[16,1408]{1,0:T(8,128)S(1)} %fusion), channel_id=1, source_target_pairs={{0,24},{2,26},{4,28},{6,30},{8,32},{10,34},{12,36},{14,38},{16,40}... | collective-permute-start | bytes 270344
  600.1 11.9 %collective-permute-start.19 = (f32[11,1408]{1,0:T(8,128)S(1)}, f32[11,1408]{1,0:T(8,128)S(1)}, u32[]{:S(2)}, u32[]{:S(2)}) collective-permute-start(f32[11,1408]{1,0:T(8,128)S(1)} %slice.30), channel_id=1, source_target_pairs={{0,40},{2,42},{4,44},{6,46},{8,48},{10,50},{12,52},{14,54},{16,56}... | collective-permute-start | bytes 185864
  612.0 9.7 collective-permute-start.12
  613.9 11.3 %collective-permute-start.13 = (f32[16,1408]{1,0:T(8,128)S(1)}, f32[16,1408]{1,0:T(8,128)S(1)}, u32[]{:S(2)}, u32[]{:S(2)}) collective-permute-start(f32[16,1408]{1,0:T(8,128)S(1)} %fusion), channel_id=1, source_target_pairs={{0,28},{2,30},{4,32},{6,34},{8,36},{10,38},{12,40},{14,42},{16,44}... | collective-permute-start | bytes 270344
  615.9 12.2 %collective-permute-start.14 = (f32[16,1408]{1,0:T(8,128)S(1)}, f32[16,1408]{1,0:T(8,128)S(1)}, u32[]{:S(2)}, u32[]{:S(2)}) collective-permute-start(f32[16,1408]{1,0:T(8,128)S(1)} %fusion), channel_id=1, source_target_pairs={{0,30},{2,32},{4,34},{6,36},{8,38},{10,40},{12,42},{14,44},{16,46}... | collective-permute-start | bytes 270344
  617.8 12.9 %collective-permute-start.15 = (f32[16,1408]{1,0:T(8,128)S(1)}, f32[16,1408]{1,0:T(8,128)S(1)}, u32[]{:S(2)}, u32[]{:S(2)}) collective-permute-start(f32[16,1408]{1,0:T(8,128)S(1)} %fusion), channel_id=1, source_target_pairs={{0,32},{2,34},{4,36},{6,38},{8,40},{10,42},{12,44},{14,46},{16,48}... | collective-permute-start | bytes 270344
  619.7 24.1 %collective-permute-start.16 = (f32[16,1408]{1,0:T(8,128)S(1)}, f32[16,1408]{1,0:T(8,128)S(1)}, u32[]{:S(2)}, u32[]{:S(2)}) collective-permute-start(f32[16,1408]{1,0:T(8,128)S(1)} %fusion), channel_id=1, source_target_pairs={{0,34},{2,36},{4,38},{6,40},{8,42},{10,44},{12,46},{14,48},{16,50}... | collective-permute-start | bytes 270344
  621.7 24.1 %collective-permute-start.17 = (f32[16,1408]{1,0:T(8,128)S(1)}, f32[16,1408]{1,0:T(8,128)S(1)}, u32[]{:S(2)}, u32[]{:S(2)}) collective-permute-start(f32[16,1408]{1,0:T(8,128)S(1)} %fusion), channel_id=1, source_target_pairs={{0,36},{2,38},{4,40},{6,42},{8,44},{10,46},{12,48},{14,50},{16,52}... | collective-permute-start | bytes 270344
  625.2 28.4 %copy-start.5 = (f32[16,1408]{1,0:T(8,128)}, f32[16,1408]{1,0:T(8,128)S(1)}, u32[]{:S(2)}) copy-start(f32[16,1408]{1,0:T(8,128)S(1)} %collective-permute-done.13) | copy-start | bytes 270340
  625.2 22.5 %collective-permute-start.18 = (f32[16,1408]{1,0:T(8,128)S(1)}, f32[16,1408]{1,0:T(8,128)S(1)}, u32[]{:S(2)}, u32[]{:S(2)}) collective-permute-start(f32[16,1408]{1,0:T(8,128)S(1)} %fusion), channel_id=1, source_target_pairs={{0,38},{2,40},{4,42},{6,44},{8,46},{10,48},{12,50},{14,52},{16,54}... | collective-permute-start | bytes 270344
  628.0 27.5 %copy-start.6 = (f32[16,1408]{1,0:T(8,128)}, f32[16,1408]{1,0:T(8,128)S(1)}, u32[]{:S(2)}) copy-start(f32[16,1408]{1,0:T(8,128)S(1)} %collective-permute-done.14) | copy-start | bytes 270340
  628.0 21.6 %collective-permute-start.2 = (f32[16,1408]{1,0:T(8,128)S(1)}, f32[16,1408]{1,0:T(8,128)S(1)}, u32[]{:S(2)}, u32[]{:S(2)}) collective-permute-start(f32[16,1408]{1,0:T(8,128)S(1)} %fusion), channel_id=1, source_target_pairs={{0,6},{2,8},{4,10},{6,12},{8,14},{10,16},{12,18},{14,20},{16,22},{... | collective-permute-start | bytes 270344
  630.7 24.8 %copy-start.7 = (f32[16,1408]{1,0:T(8,128)}, f32[16,1408]{1,0:T(8,128)S(1)}, u32[]{:S(2)}) copy-start(f32[16,1408]{1,0:T(8,128)S(1)} %collective-permute-done.15) | copy-start | bytes 270340
  630.7 20.9 %collective-permute-start.3 = (f32[16,1408]{1,0:T(8,128)S(1)}, f32[16,1408]{1,0:T(8,128)S(1)}, u32[]{:S(2)}, u32[]{:S(2)}) collective-permute-start(f32[16,1408]{1,0:T(8,128)S(1)} %fusion), channel_id=1, source_target_pairs={{0,8},{2,10},{4,12},{6,14},{8,16},{10,18},{12,20},{14,22},{16,24},... | collective-permute-start | bytes 270344
  643.8 11.7 %copy-start.8 = (f32[16,1408]{1,0:T(8,128)}, f32[16,1408]{1,0:T(8,128)S(1)}, u32[]{:S(2)}) copy-start(f32[16,1408]{1,0:T(8,128)S(1)} %collective-permute-done.16) | copy-start | bytes 270340
  643.8 9.7 collective-permute-start.4
  645.8 9.8 copy-start.9
  645.8 11.9 %collective-permute-start.5 = (f32[16,1408]{1,0:T(8,128)S(1)}, f32[16,1408]{1,0:T(8,128)}, u32[]{:S(2)}, u32[]{:S(2)}) collective-permute-start(f32[16,1408]{1,0:T(8,128)S(1)} %fusion), channel_id=1, source_target_pairs={{0,12},{2,14},{4,16},{6,18},{8,20},{10,22},{12,24},{14,26},{16,28}... | collective-permute-start | bytes 270344
  647.7 7.8 copy-start.10
  647.7 10.0 collective-permute-start.6
  649.7 5.9 copy-start.11
  649.7 11.4 %collective-permute-start.7 = (f32[16,1408]{1,0:T(8,128)S(1)}, f32[16,1408]{1,0:T(8,128)}, u32[]{:S(2)}, u32[]{:S(2)}) collective-permute-start(f32[16,1408]{1,0:T(8,128)S(1)} %fusion), channel_id=1, source_target_pairs={{0,16},{2,18},{4,20},{6,22},{8,24},{10,26},{12,28},{14,30},{16,32}... | collective-permute-start | bytes 270344
  651.6 4.0 copy-start.12
  651.6 12.8 %collective-permute-start.8 = (f32[16,1408]{1,0:T(8,128)S(1)}, f32[16,1408]{1,0:T(8,128)}, u32[]{:S(2)}, u32[]{:S(2)}) collective-permute-start(f32[16,1408]{1,0:T(8,128)S(1)} %fusion), channel_id=1, source_target_pairs={{0,18},{2,20},{4,22},{6,24},{8,26},{10,28},{12,30},{14,32},{16,34}... | collective-permute-start | bytes 270344
  653.6 2.0 copy-start.13
  653.6 13.4 %collective-permute-start.9 = (f32[16,1408]{1,0:T(8,128)S(1)}, f32[16,1408]{1,0:T(8,128)}, u32[]{:S(2)}, u32[]{:S(2)}) collective-permute-start(f32[16,1408]{1,0:T(8,128)S(1)} %fusion), channel_id=1, source_target_pairs={{0,20},{2,22},{4,24},{6,26},{8,28},{10,30},{12,32},{14,34},{16,36}... | collective-permute-start | bytes 270344
Sparse Core Ops, SparseCore 0:
  400.3 105.0 reduce-scatter.4
Sparse Core Ops, SparseCore 1:
  415.8 596.6 all-reduce.4
where the time goes:
time: 1030 us
  blocking collectives  379 us (37%)
  waiting for transfers between devices  330 us (32%)
  local copies, waits for them, and re-layouts  139 us (13%)
  matrix products  95.2 us (9%)
  starting transfers between devices  50.6 us (5%)
  between operations  17.7 us (2%)
  other arithmetic  14.3 us (1%)
    unnamed x23, waiting for transfers between devices  330 us
    unnamed x1, blocking collectives  170 us
    all_to_all x1, blocking collectives, shards(): lax.all_to_all(stacked, 'seq', split_axis=1, concat_axis=0, tiled=True)  106 us
    all_to_all x1, blocking collectives, shards(): lax.all_to_all(result, 'seq', split_axis=0, concat_axis=1, tiled=True)  103 us
    unnamed x42, local copies, waits for them, and re-layouts  58.5 us
    unnamed x21, starting transfers between devices  50.5 us
    reshape x2, local copies, waits for them, and re-layouts, shards(): stacked = stacked.reshape(frames_here, P_SIZE, 4, heads_here, HEAD_DIM)  25.8 us
  transfers between devices with their start and end apart: 22, of which 8 were waited for; matrix products, arithmetic and copies ran while one was open for 22% of the time, Pallas kernels for 0%

commit v1 on v0

v1 whole, which is shorter than its diff:
```python
import functools

import jax
import jax.numpy as jnp
from jax import lax
from jax.experimental import pallas as pl
from jax.experimental.pallas import tpu as pltpu
from jax.sharding import PartitionSpec as P

HEAD_DIM = 88
P_SIZE = 256
MIB = 1024 * 1024
BF = jnp.bfloat16
F32 = jnp.float32
NN = (((1,), (0,)), ((), ()))
NT = (((1,), (1,)), ((), ()))
TN = (((0,), (0,)), ((), ()))


def mm(a, b, dims=NN):
    return lax.dot_general(a, b, dims, preferred_element_type=F32)


def onehot(rows, cols, match):
    r = lax.broadcasted_iota(jnp.int32, (rows, cols), 0)
    c = lax.broadcasted_iota(jnp.int32, (rows, cols), 1)
    return jnp.where(match(r, c), 1.0, 0.0).astype(BF)


def params(mib):
    return pltpu.CompilerParams(vmem_limit_bytes=mib * MIB)


def pack_kernel(x_ref, o_ref):
    width = x_ref.shape[2]
    perm = onehot(
        256,
        256,
        lambda r, c: ((r >> 4) == ((c >> 2) & 15)) & (((r >> 2) & 3) == (c & 3)) & ((r & 3) == (c >> 6)),
    )
    o_ref[...] = mm(perm, x_ref[...].reshape(256, width)).astype(BF)


def pack(x):
    tokens, width = x.shape
    return pl.pallas_call(
        pack_kernel,
        grid=(4,),
        in_specs=[pl.BlockSpec((4, 64, width), lambda b: (0, b, 0))],
        out_specs=pl.BlockSpec((256, width), lambda b: (b, 0)),
        out_shape=jax.ShapeDtypeStruct((tokens, width), BF),
        compiler_params=params(16),
        cost_estimate=pl.CostEstimate(flops=2 * tokens * 256 * width, bytes_accessed=4 * tokens * width, transcendentals=0),
        name="pack_rows",
    )(x.reshape(4, P_SIZE, width))


def by_patch(x_ref, sorted_ref):
    perm = onehot(
        256,
        256,
        lambda r, c: ((r >> 6) == ((c >> 2) & 3)) & (((r >> 2) & 15) == (c >> 4)) & ((r & 3) == (c & 3)),
    )
    for b in range(4):
        part = mm(perm, x_ref[b * 256 : (b + 1) * 256, :]).astype(BF)
        for p in range(4):
            sorted_ref[p, b * 64 : (b + 1) * 64, :] = part[p * 64 : (p + 1) * 64, :]


def forward_kernel(x_ref, w_ref, xt_ref, qkv_ref, prob_ref, attn_ref, sorted_ref):
    heads = qkv_ref.shape[1] // 3
    local = heads * HEAD_DIM
    scale = HEAD_DIM ** -0.5

    @pl.when(pl.program_id(0) == 0)
    def _():
        by_patch(x_ref, sorted_ref)

    xt = sorted_ref[pl.program_id(0)].T
    xt_ref[...] = xt
    for j in range(3):
        part = mm(w_ref[j * local : (j + 1) * local, :], xt)
        qkv_ref[0, j * heads : (j + 1) * heads] = part.reshape(heads, HEAD_DIM, 256).astype(BF)
    for h in range(heads):
        query = qkv_ref[0, h]
        key = qkv_ref[0, heads + h]
        value = qkv_ref[0, 2 * heads + h]
        scores = mm(key.T, query) * scale
        expo = jnp.exp(scores - jnp.max(scores, axis=0, keepdims=True))
        prob = expo / jnp.sum(expo, axis=0, keepdims=True)
        prob_ref[0, h] = prob
        attn_ref[0, h] = mm(value, prob.astype(BF)).astype(BF)


def forward(x, w):
    tokens, width = x.shape
    heads = w.shape[0] // 3 // HEAD_DIM
    return pl.pallas_call(
        forward_kernel,
        grid=(4,),
        in_specs=[
            pl.BlockSpec((tokens, width), lambda p: (0, 0)),
            pl.BlockSpec(w.shape, lambda p: (0, 0)),
        ],
        out_specs=[
            pl.BlockSpec((width, 256), lambda p: (0, p)),
            pl.BlockSpec((1, 3 * heads, HEAD_DIM, 256), lambda p: (p, 0, 0, 0)),
            pl.BlockSpec((1, heads, 256, 256), lambda p: (p, 0, 0, 0)),
            pl.BlockSpec((1, heads, HEAD_DIM, 256), lambda p: (p, 0, 0, 0)),
        ],
        out_shape=[
            jax.ShapeDtypeStruct((width, tokens), BF),
            jax.ShapeDtypeStruct((4, 3 * heads, HEAD_DIM, 256), BF),
            jax.ShapeDtypeStruct((4, heads, 256, 256), F32),
            jax.ShapeDtypeStruct((4, heads, HEAD_DIM, 256), BF),
        ],
        scratch_shapes=[pltpu.VMEM((4, 256, width), BF)],
        compiler_params=params(48),
        cost_estimate=pl.CostEstimate(flops=9 * 10**9, bytes_accessed=24 * 10**6, transcendentals=4 * heads * 65536),
        name="forward",
    )(x, w)


def backward_kernel(c_ref, wo_ref, w_ref, qkv_ref, prob_ref, sorted_ref, dqkv_ref, send_ref, grad_ref, cotangent_ref, total_ref):
    heads = prob_ref.shape[1]
    local = heads * HEAD_DIM
    scale = HEAD_DIM ** -0.5
    p = pl.program_id(0)

    @pl.when(p == 0)
    def _():
        by_patch(c_ref, sorted_ref)

    grad = mm(wo_ref[...], sorted_ref[p], NT)
    grad_ref[...] = grad.reshape(heads, HEAD_DIM, 256).astype(BF)
    for h in range(heads):
        query = qkv_ref[0, h]
        key = qkv_ref[0, heads + h]
        value = qkv_ref[0, 2 * heads + h]
        gout = grad_ref[h]
        prob = prob_ref[0, h]
        dvalue = mm(gout, prob.astype(BF), NT)
        dweights = mm(value.T, gout)
        mean = jnp.sum(prob * dweights, axis=0, keepdims=True)
        dscores = (prob * (dweights - mean) * scale).astype(BF)
        dquery = mm(key, dscores)
        dkey = mm(query, dscores, NT)
        cotangent_ref[h] = dquery.astype(BF)
        cotangent_ref[heads + h] = dkey.astype(BF)
        cotangent_ref[2 * heads + h] = dvalue.astype(BF)
    dqkv = cotangent_ref[...].astype(F32).reshape(3 * local, 256).astype(BF)
    dqkv_ref[...] = dqkv
    total_ref[p] = mm(w_ref[...], dqkv).astype(BF)

    @pl.when(p == 3)
    def _():
        perm = onehot(
            512,
            512,
            lambda r, c: (((r >> 2) & 3) == (c >> 7)) & ((r >> 4) == ((c >> 2) & 31)) & ((r & 3) == (c & 3)),
        )
        half = total_ref.shape[1] // 2
        for b in range(2):
            for t in range(2):
                cols = jnp.concatenate(
                    [total_ref[q, t * half : (t + 1) * half, b * 128 : (b + 1) * 128] for q in range(4)], axis=1
                )
                part = mm(perm, cols, NT).astype(BF)
                send_ref[b * 32 : (b + 1) * 32, t] = part.reshape(32, 16, half)


def backward(cot, wo, w, qkv, prob):
    tokens, width = cot.shape
    heads = prob.shape[1]
    local = heads * HEAD_DIM
    return pl.pallas_call(
        backward_kernel,
        grid=(4,),
        in_specs=[
            pl.BlockSpec((tokens, width), lambda p: (0, 0)),
            pl.BlockSpec(wo.shape, lambda p: (0, 0)),
            pl.BlockSpec(w.shape, lambda p: (0, 0)),
            pl.BlockSpec((1, 3 * heads, HEAD_DIM, 256), lambda p: (p, 0, 0, 0)),
            pl.BlockSpec((1, heads, 256, 256), lambda p: (p, 0, 0, 0)),
        ],
        out_specs=[
            pl.BlockSpec((4, 256, width), lambda p: (0, 0, 0)),
            pl.BlockSpec((3 * local, 256), lambda p: (0, p)),
            pl.BlockSpec((64, 2, 16, width // 2), lambda p: (0, 0, 0, 0)),
        ],
        out_shape=[
            jax.ShapeDtypeStruct((4, 256, width), BF),
            jax.ShapeDtypeStruct((3 * local, tokens), BF),
            jax.ShapeDtypeStruct((64, 2, 16, width // 2), BF),
        ],
        scratch_shapes=[
            pltpu.VMEM((heads, HEAD_DIM, 256), BF),
            pltpu.VMEM((3 * heads, HEAD_DIM, 256), BF),
            pltpu.VMEM((4, width, 256), BF),
        ],
        compiler_params=params(56),
        cost_estimate=pl.CostEstimate(flops=12 * 10**9, bytes_accessed=30 * 10**6, transcendentals=0),
        name="backward",
    )(cot, wo, w, qkv, prob)


def weights_kernel(core_ref, xt_ref, dqkv_ref, attn_ref, c_ref, o_ref):
    core = core_ref[0]
    width = xt_ref.shape[0]
    local = attn_ref.shape[0]
    cols = dqkv_ref.shape[0]
    step = pl.program_id(0)
    rows = o_ref.shape[0] * 24

    def device_row(r):
        place = r // 24
        return place, r - place * 24

    r = lax.broadcasted_iota(jnp.int32, (rows, width), 0) + step * rows
    place, at = device_row(r)
    f = lax.broadcasted_iota(jnp.int32, (rows, width), 1)
    pick = jnp.where((f == (2 * place + core) * 22 + at) & (at < 22), 1.0, 0.0).astype(BF)
    left = mm(pick, xt_ref[...]).astype(BF)
    o_ref[:, :, :cols] = mm(left, dqkv_ref[...], NT).astype(BF).reshape(rows // 24, 24, cols)
    r = lax.broadcasted_iota(jnp.int32, (rows, local), 0) + step * rows
    place, at = device_row(r)
    c = lax.broadcasted_iota(jnp.int32, (rows, local), 1)
    first = (2 * place + core) * 11
    low = jnp.where((c == first + at) & (at < 11), 1.0, 0.0).astype(BF)
    high = jnp.where((c == first + at - 11) & (at >= 11) & (at < 22), 1.0, 0.0).astype(BF)
    half = width // 2
    total = mm(mm(low, attn_ref[...]).astype(BF), c_ref[:, :half])
    total += mm(mm(high, attn_ref[...]).astype(BF), c_ref[:, half:])
    o_ref[:, :, cols:] = total.astype(BF).reshape(rows // 24, 24, half)


def weight_grads(core, xt, dqkv, attn, cot):
    width, tokens = xt.shape
    cols = dqkv.shape[0]
    local = attn.shape[0]
    whole = lambda a: pl.BlockSpec(a.shape, lambda s: (0,) * a.ndim)
    return pl.pallas_call(
        weights_kernel,
        grid=(4,),
        in_specs=[pl.BlockSpec(memory_space=pltpu.SMEM), whole(xt), whole(dqkv), whole(attn), whole(cot)],
        out_specs=pl.BlockSpec((8, 24, cols + width // 2), lambda s: (s, 0, 0)),
        out_shape=jax.ShapeDtypeStruct((32, 24, cols + width // 2), BF),
        compiler_params=params(56),
        cost_estimate=pl.CostEstimate(flops=8 * 10**9, bytes_accessed=24 * 10**6, transcendentals=0),
        name="weight_grads",
    )(core, xt, dqkv, attn, cot)


def unpack_kernel(x_ref, o_ref):
    half = x_ref.shape[2]
    pick = onehot(
        1024,
        512,
        lambda r, c: ((r & 3) == (c >> 7)) & ((r >> 5) == ((c >> 2) & 31)) & (((r >> 2) & 3) == (c & 3)),
    )
    for b in range(2):
        rows = x_ref[b * 64 : (b + 1) * 64].reshape(1024, half)
        part = mm(rows.T, pick).astype(BF)
        for f in range(4):
            o_ref[:, f * 256 + b * 128 : f * 256 + (b + 1) * 128] = part[:, f * 128 : (f + 1) * 128]


def unpack(x):
    half = x.shape[2]
    return pl.pallas_call(
        unpack_kernel,
        out_shape=jax.ShapeDtypeStruct((half, 1024), BF),
        compiler_params=params(32),
        cost_estimate=pl.CostEstimate(flops=2 * half * 1024 * 1024, bytes_accessed=5 * 10**6, transcendentals=0),
        name="unpack_rows",
    )(x)


def shards(hidden, out_cotangent, qkv_weight, out_weight):
    tokens, width = hidden.shape
    local = qkv_weight.shape[2]
    n_seq = lax.axis_size("seq")
    w_rows = qkv_weight.transpose(1, 2, 0).reshape(3 * local, width)
    w_cols = qkv_weight.reshape(width, 3 * local)

    def to_patches(rows):
        return lax.all_to_all(rows.reshape(n_seq, 16, width), "seq", split_axis=0, concat_axis=0, tiled=True).reshape(tokens, width)

    hidden_in = to_patches(pack(hidden))
    cot_send = pack(out_cotangent)
    hidden_in, cot_send, w_cols = lax.optimization_barrier((hidden_in, cot_send, w_cols))
    cot_in = to_patches(cot_send)
    xt, qkv, prob, attn = forward(hidden_in, w_rows)
    cot_rows, dqkv, send = backward(cot_in, out_weight, w_cols, qkv, prob)
    attn = attn.transpose(1, 2, 0, 3).reshape(local, tokens)
    cot_rows = cot_rows.reshape(tokens, width)

    returned = lax.all_to_all(send.reshape(2 * n_seq, 16, width // 2), ("seq", "tp"), split_axis=0, concat_axis=0, tiled=True)
    core = lax.axis_index("seq") % 2
    grads = functools.partial(weight_grads, xt=xt, dqkv=dqkv, attn=attn, cot=cot_rows)
    other = grads((1 - core).reshape(1).astype(jnp.int32))
    arrived = lax.ppermute(other, "seq", [(i, i ^ 1) for i in range(n_seq)])
    mine = grads(core.reshape(1).astype(jnp.int32))
    chip = (mine.astype(F32) + arrived.astype(F32)).astype(BF)
    returned, chip = lax.optimization_barrier((returned, chip))
    groups = [list(range(0, n_seq, 2)), list(range(1, n_seq, 2))]
    terms = lax.all_to_all(chip, "seq", split_axis=0, concat_axis=0, tiled=True, axis_index_groups=groups)
    grad_hidden = unpack(returned).T
    total = terms.astype(F32).sum(0)
    qkv_grad = total[:22, : 3 * local].reshape(22, 3, local)
    out_grad = total[:22, 3 * local :].reshape(2, 11, width // 2).transpose(1, 0, 2).reshape(11, width)
    return (grad_hidden, qkv_grad, out_grad)


def solution(mesh):
    return jax.shard_map(
        shards,
        mesh=mesh,
        in_specs=(P("seq", None), P("seq", None), P(None, None, "tp"), P("tp", None)),
        out_specs=(P("seq", "tp"), P("seq", None, "tp"), P(("tp", "seq"), None)),
        check_vma=False,
    )
```

time: 1030 us -> 278 us (0.27)
  blocking collectives: 379 us -> 0 us
  waiting for transfers between devices: 330 us -> 104 us
  local copies, waits for them, and re-layouts: 139 us -> 17.1 us
  Pallas kernels: 0 us -> 109 us
  matrix products: 95.2 us -> 0 us
  between operations: 17.7 us -> 0.73 us
  starting transfers between devices: 50.6 us -> 34.5 us
    unnamed x23 -> x0, waiting for transfers between devices: 330 us -> none
    all_to_all x2 -> x0, blocking collectives: 209 us -> none  [the longest x1 106 us: shards(): lax.all_to_all(stacked, 'seq', split_axis=1, concat_axis=0, tiled=True)]
    unnamed x1 -> x0, blocking collectives: 170 us -> none
    pallas_call x0 -> x7, Pallas kernels: none -> 109 us  [the longest x2 41 us: weight_grads(): pl.pallas_call(weights_kernel, grid=(4,), in_specs=[pl.BlockSpec(memory_s...]
    all_to_all x0 -> x4, waiting for transfers between devices: none -> 104 us  [the longest x1 56.9 us: shards(): lax.all_to_all(chip, 'seq', split_axis=0, concat_axis=0, tiled=True, axis...]
    dot_general x11 -> x0, matrix products: 95.2 us -> none  [the longest x1 15.5 us: shards(): jnp.einsum('tc,tf->cf', columns, dqkv, preferred_element_type=jnp.float32)]
    unnamed x42 -> x10, local copies, waits for them, and re-layouts: 58.5 us -> 5.94 us
    unnamed x21 -> x0, starting transfers between devices: 50.5 us -> none
  transfers between devices with their start and end apart: 22 -> 5, of which waited for: 8 -> 4; matrix products, arithmetic and copies ran while one was open for 22% -> 7% of each run, Pallas kernels for 0% -> 19%
where the time goes in v1:
time: 278 us; the launch traced here: 275 us
  Pallas kernels  109 us (39%)
  waiting for transfers between devices  104 us (37%)
  starting transfers between devices  34.5 us (12%)
  local copies, waits for them, and re-layouts  17.1 us (6%)
  other arithmetic  9.52 us (3%)
    all_to_all x1, waiting for transfers between devices, shards(): lax.all_to_all(chip, 'seq', split_axis=0, concat_axis=0, tiled=True, axis...  56.9 us
    pallas_call x2, Pallas kernels, weight_grads(): pl.pallas_call(weights_kernel, grid=(4,), in_specs=[pl.BlockSpec(memory_s...  41 us
    all_to_all x2, waiting for transfers between devices, to_patches(): lax.all_to_all(rows.reshape(n_seq, 16, width), 'seq', split_axis=0, conca...  34.5 us
    pallas_call x1, Pallas kernels, backward(): pl.pallas_call(backward_kernel, grid=(4,), in_specs=[pl.BlockSpec((tokens...  34.1 us
    pallas_call x1, Pallas kernels, forward(): pl.pallas_call(forward_kernel, grid=(4,), in_specs=[pl.BlockSpec((tokens,...  24.5 us
    all_to_all x2, starting transfers between devices, to_patches(): lax.all_to_all(rows.reshape(n_seq, 16, width), 'seq', split_axis=0, conca...  17.9 us
    all_to_all x1, waiting for transfers between devices, shards(): lax.all_to_all(send.reshape(2 * n_seq, 16, width // 2), ('seq', 'tp'), sp...  13.1 us
    all_to_all x1, starting transfers between devices, shards(): lax.all_to_all(send.reshape(2 * n_seq, 16, width // 2), ('seq', 'tp'), sp...  10.5 us
  transfers between devices with their start and end apart: 5, of which 4 were waited for; matrix products, arithmetic and copies ran while one was open for 7% of the time, Pallas kernels for 19%

profile of v1, /device:TPU:32, one launch (start us, length us, event | category | flops | bytes accessed | tf_op | source)
XLA Modules:
  0.0 275.1 jit_solution(7498575389736976082)
XLA Ops:
  0.6 0.0 copy-start
  0.6 1.8 copy-done
  2.4 3.1 %pack_rows.2 = bf16[1024,1408]{1,0:T(8,128)(2,1)} custom-call(bf16[4,256,1408]{2,1,0:T(8,128)(2,1)S(1)} %bitcast.20), custom_call_target="tpu_custom_call" | custom-call | flops 738197504 | bytes 5767168 | tf_op jit(solution)/shard_map/pack_rows/pallas_call | solution.py:46
  5.5 0.0 copy-start.1
  5.5 9.5 %all-to-all-start = ((bf16[64,16,1408]{2,1,0:T(8,128)(2,1)}), bf16[64,16,1408]{2,1,0:T(8,128)(2,1)}, u32[]{:S(2)}, u32[]{:S(2)}) async-start(bf16[64,16,1408]{2,1,0:T(8,128)(2,1)} %bitcast.1), calls=%async_computation | async-start | bytes 5767168 | tf_op jit(solution)/shard_map/all_to_all | solution.py:287
  15.0 0.0 copy-done.1
  15.0 3.2 %pack_rows.3 = bf16[1024,1408]{1,0:T(8,128)(2,1)} custom-call(bf16[4,256,1408]{2,1,0:T(8,128)(2,1)S(1)} %bitcast.21), custom_call_target="tpu_custom_call" | custom-call | flops 738197504 | bytes 5767168 | tf_op jit(solution)/shard_map/pack_rows/pallas_call | solution.py:46
  18.2 33.8 %all-to-all-done = bf16[64,16,1408]{2,1,0:T(8,128)(2,1)} async-done(((bf16[64,16,1408]{2,1,0:T(8,128)(2,1)}), bf16[64,16,1408]{2,1,0:T(8,128)(2,1)}, u32[]{:S(2)}, u32[]{:S(2)}) %all-to-all-start) | async-done | bytes 2883616 | tf_op jit(solution)/shard_map/all_to_all | solution.py:287
  52.0 8.4 %all-to-all-start.1 = ((bf16[64,16,1408]{2,1,0:T(8,128)(2,1)}), bf16[64,16,1408]{2,1,0:T(8,128)(2,1)S(1)}, u32[]{:S(2)}, u32[]{:S(2)}) async-start(bf16[64,16,1408]{2,1,0:T(8,128)(2,1)} %bitcast.5), calls=%async_computation.1 | async-start | bytes 5767168 | tf_op jit(solution)/shard_map/all_to_all | solution.py:287
  60.5 8.9 %copy.12.w_ref = bf16[1408,2112]{1,0:T(8,128)(2,1)} copy(bf16[1408,2112]{0,1:T(8,128)(2,1)} %bitcast.23) | data formatting | bytes 11894784 | tf_op jit(solution)/shard_map/optimization_barrier | solution.py:291
  69.4 24.5 %forward.1 = (bf16[1408,1024]{1,0:T(8,128)(2,1)S(1)}, bf16[4,24,88,256]{3,2,1,0:T(8,128)(2,1)}, f32[4,8,256,256]{3,2,1,0:T(8,128)}, bf16[4,8,88,256]{3,2,1,0:T(8,128)(2,1)S(1)}) custom-call(bf16[1024,1408]{1,0:T(8,128)(2,1)} %bitcast.2.x_ref, bf16[2112,1408]{1,0:T(8,128)(2,1)} %bitcast.24), custom_call_target="tpu_custom_call" | custom-call | flops 8999999488 | bytes 24000000 | tf_op jit(solution)/shard_map/forward/pallas_call | solution.py:98
  93.9 0.0 copy-start.2
  93.9 1.1 copy.13
  95.0 0.4 copy-done.2
  95.4 1.4 copy.16
  96.8 0.7 all-to-all-done.1
  97.5 0.0 copy-start.3
  97.6 1.5 copy-done.3
  99.1 34.1 %backward.1 = (bf16[4,256,1408]{2,1,0:T(8,128)(2,1)}, bf16[2112,1024]{1,0:T(8,128)(2,1)}, bf16[64,2,16,704]{3,2,1,0:T(8,128)(2,1)}) custom-call(bf16[1024,1408]{1,0:T(8,128)(2,1)} %bitcast.27, bf16[704,1408]{1,0:T(8,128)(2,1)} %wo_ref.1, bf16[1408,2112]{1,0:T(8,128)(2,1)} %copy.12.w_ref, bf16[4,24,88,256]{3,2,1,0:T(8,128)(2,1)} %get-tuple-element.18.qkv_ref, ...), custom_call_target="tpu_custom_call" | custom-call | flops 12000000000 | bytes 30000000 | tf_op jit(solution)/shard_map/backward/pallas_call | solution.py:176
  133.2 20.5 %weight_grads.3 = bf16[32,24,2816]{2,1,0:T(8,128)(2,1)} custom-call(s32[1]{0:T(128)} %bitcast.13.core_ref, bf16[1408,1024]{1,0:T(8,128)(2,1)} %copy-done.2, bf16[2112,1024]{1,0:T(8,128)(2,1)} %get-tuple-element.22.dqkv_ref, bf16[704,1024]{1,0:T(8,128)(2,1)} %bitcast.28, bf16[1024,1408]{1,0:T(8,128)(2,1)} %bitcast.31), custom_call_target="tpu_custom_call" | custom-call | flops 8000000000 | bytes 24000000 | tf_op jit(solution)/shard_map/weight_grads/pallas_call | solution.py:242
  153.8 0.1 collective-permute-start
  153.9 10.5 %all-to-all-start.2 = ((bf16[128,16,704]{2,1,0:T(8,128)(2,1)}), bf16[128,16,704]{2,1,0:T(8,128)(2,1)S(1)}, u32[]{:S(2)}, u32[]{:S(2)}) async-start(bf16[128,16,704]{2,1,0:T(8,128)(2,1)} %bitcast.26), calls=%async_computation.2 | async-start | bytes 6291456 | tf_op jit(solution)/shard_map/all_to_all | solution.py:298
  164.4 20.5 %weight_grads.2 = bf16[32,24,2816]{2,1,0:T(8,128)(2,1)} custom-call(s32[1]{0:T(128)} %bitcast.10.core_ref, bf16[1408,1024]{1,0:T(8,128)(2,1)} %copy-done.2, bf16[2112,1024]{1,0:T(8,128)(2,1)} %get-tuple-element.22.dqkv_ref, bf16[704,1024]{1,0:T(8,128)(2,1)} %bitcast.29, bf16[1024,1408]{1,0:T(8,128)(2,1)} %bitcast.32), custom_call_target="tpu_custom_call" | custom-call | flops 8000000000 | bytes 24000000 | tf_op jit(solution)/shard_map/weight_grads/pallas_call | solution.py:242
  184.8 0.0 collective-permute-done
  184.8 6.6 %add_convert_fusion = bf16[32,24,2816]{2,1,0:T(8,128)(2,1)} fusion(bf16[32,24,2816]{2,1,0:T(8,128)(2,1)} %collective-permute-done, bf16[32,24,2816]{2,1,0:T(8,128)(2,1)} %weight_grads.2), kind=kLoop, calls=%fused_computation.1 | loop fusion | flops 8650752 | bytes 12976128 | tf_op jit(solution)/shard_map/convert_element_type | solution.py:304
  191.5 13.1 %all-to-all-done.2.x_ref = bf16[128,16,704]{2,1,0:T(8,128)(2,1)S(1)} async-done(((bf16[128,16,704]{2,1,0:T(8,128)(2,1)}), bf16[128,16,704]{2,1,0:T(8,128)(2,1)S(1)}, u32[]{:S(2)}, u32[]{:S(2)}) %all-to-all-start.2) | async-done | bytes 2883616 | tf_op jit(solution)/shard_map/all_to_all | solution.py:298
  204.5 6.1 %all-to-all-start.3 = ((bf16[32,24,2816]{2,1,0:T(8,128)(2,1)}), bf16[32,24,2816]{2,1,0:T(8,128)(2,1)}, u32[]{:S(2)}, u32[]{:S(2)}) async-start(bf16[32,24,2816]{2,1,0:T(8,128)(2,1)} %add_convert_fusion), calls=%async_computation.3 | async-start | bytes 8650752 | tf_op jit(solution)/shard_map/all_to_all | solution.py:307
  210.6 2.9 %unpack_rows.1 = bf16[704,1024]{1,0:T(8,128)(2,1)} custom-call(bf16[128,16,704]{2,1,0:T(8,128)(2,1)S(1)} %all-to-all-done.2.x_ref), custom_call_target="tpu_custom_call" | custom-call | flops 1476395008 | bytes 5000000 | tf_op jit(solution)/shard_map/unpack_rows/pallas_call | solution.py:270
  213.5 56.9 %all-to-all-done.3 = bf16[32,24,2816]{2,1,0:T(8,128)(2,1)} async-done(((bf16[32,24,2816]{2,1,0:T(8,128)(2,1)}), bf16[32,24,2816]{2,1,0:T(8,128)(2,1)}, u32[]{:S(2)}, u32[]{:S(2)}) %all-to-all-start.3) | async-done | bytes 4325408 | tf_op jit(solution)/shard_map/all_to_all | solution.py:307
  270.4 2.9 %convert_reduce_fusion = f32[24,2816]{1,0:T(8,128)S(1)} fusion(bf16[32,24,2816]{2,1,0:T(8,128)(2,1)} %all-to-all-done.3), kind=kLoop, calls=%fused_computation | loop fusion | flops 4257792 | bytes 4595712 | tf_op jit(solution)/shard_map/reduce_sum | solution.py:309
  273.3 0.1 slice.9
  273.4 0.2 reshape.67
  273.5 0.7 copy.15
  274.3 0.1 copy.14
  274.3 0.8 reshape.69
  (2 shorter events, 0.0 us)
Async XLA Ops:
  0.6 1.8 copy-start
  5.5 9.5 %copy-start.1 = (bf16[1024,1408]{1,0:T(8,128)(2,1)S(1)}, bf16[1024,1408]{1,0:T(8,128)(2,1)}, u32[]{:S(2)}) copy-start(bf16[1024,1408]{1,0:T(8,128)(2,1)} %param.5) | copy-start | bytes 8650756
  5.5 46.5 %all-to-all-start = ((bf16[64,16,1408]{2,1,0:T(8,128)(2,1)}), bf16[64,16,1408]{2,1,0:T(8,128)(2,1)}, u32[]{:S(2)}, u32[]{:S(2)}) async-start(bf16[64,16,1408]{2,1,0:T(8,128)(2,1)} %bitcast.1), calls=%async_computation | async-start | bytes 5767168 | tf_op jit(solution)/shard_map/all_to_all | solution.py:287
  52.0 45.5 %all-to-all-start.1 = ((bf16[64,16,1408]{2,1,0:T(8,128)(2,1)}), bf16[64,16,1408]{2,1,0:T(8,128)(2,1)S(1)}, u32[]{:S(2)}, u32[]{:S(2)}) async-start(bf16[64,16,1408]{2,1,0:T(8,128)(2,1)} %bitcast.5), calls=%async_computation.1 | async-start | bytes 5767168 | tf_op jit(solution)/shard_map/all_to_all | solution.py:287
  93.9 1.6 copy-start.2
  97.5 1.5 copy-start.3
  153.8 31.1 %collective-permute-start = (bf16[32,24,2816]{2,1,0:T(8,128)(2,1)}, bf16[32,24,2816]{2,1,0:T(8,128)(2,1)}, u32[]{:S(2)}, u32[]{:S(2)}) collective-permute-start(bf16[32,24,2816]{2,1,0:T(8,128)(2,1)} %weight_grads.3), channel_id=1, source_target_pairs={{0,2},{2,0},{4,6},{6,4},{8,10},{10,8},{12,14},{14,12},{16,18},{18,... | collective-permute-start | bytes 12976136 | tf_op jit(solution)/shard_map/ppermute | solution.py:302
  153.9 50.6 %all-to-all-start.2 = ((bf16[128,16,704]{2,1,0:T(8,128)(2,1)}), bf16[128,16,704]{2,1,0:T(8,128)(2,1)S(1)}, u32[]{:S(2)}, u32[]{:S(2)}) async-start(bf16[128,16,704]{2,1,0:T(8,128)(2,1)} %bitcast.26), calls=%async_computation.2 | async-start | bytes 6291456 | tf_op jit(solution)/shard_map/all_to_all | solution.py:298
  204.5 65.8 %all-to-all-start.3 = ((bf16[32,24,2816]{2,1,0:T(8,128)(2,1)}), bf16[32,24,2816]{2,1,0:T(8,128)(2,1)}, u32[]{:S(2)}, u32[]{:S(2)}) async-start(bf16[32,24,2816]{2,1,0:T(8,128)(2,1)} %add_convert_fusion), calls=%async_computation.3 | async-start | bytes 8650752 | tf_op jit(solution)/shard_map/all_to_all | solution.py:307

commit v2 on v1

v2 whole, which is shorter than its diff:
```python
import functools

import jax
import jax.numpy as jnp
from jax import lax
from jax.experimental import pallas as pl
from jax.experimental.pallas import tpu as pltpu
from jax.sharding import PartitionSpec as P

HEAD_DIM = 88
P_SIZE = 256
MIB = 1024 * 1024
BF = jnp.bfloat16
F32 = jnp.float32
NN = (((1,), (0,)), ((), ()))
NT = (((1,), (1,)), ((), ()))
TN = (((0,), (0,)), ((), ()))


def mm(a, b, dims=NN):
    return lax.dot_general(a, b, dims, preferred_element_type=F32)


def onehot(rows, cols, match):
    r = lax.broadcasted_iota(jnp.int32, (rows, cols), 0)
    c = lax.broadcasted_iota(jnp.int32, (rows, cols), 1)
    return jnp.where(match(r, c), 1.0, 0.0).astype(BF)


def params(mib):
    return pltpu.CompilerParams(vmem_limit_bytes=mib * MIB)


def pack_kernel(x_ref, o_ref):
    width = x_ref.shape[2]
    perm = onehot(
        256,
        256,
        lambda r, c: ((r >> 4) == ((c >> 2) & 15)) & (((r >> 2) & 3) == (c & 3)) & ((r & 3) == (c >> 6)),
    )
    o_ref[...] = mm(perm, x_ref[...].reshape(256, width)).astype(BF)


def pack(x):
    tokens, width = x.shape
    return pl.pallas_call(
        pack_kernel,
        grid=(4,),
        in_specs=[pl.BlockSpec((4, 64, width), lambda b: (0, b, 0))],
        out_specs=pl.BlockSpec((256, width), lambda b: (b, 0)),
        out_shape=jax.ShapeDtypeStruct((tokens, width), BF),
        compiler_params=params(16),
        cost_estimate=pl.CostEstimate(flops=2 * tokens * 256 * width, bytes_accessed=4 * tokens * width, transcendentals=0),
        name="pack_rows",
    )(x.reshape(4, P_SIZE, width))


def by_patch(x_ref, sorted_ref):
    perm = onehot(
        256,
        256,
        lambda r, c: ((r >> 6) == ((c >> 2) & 3)) & (((r >> 2) & 15) == (c >> 4)) & ((r & 3) == (c & 3)),
    )
    for b in range(4):
        part = mm(perm, x_ref[b * 256 : (b + 1) * 256, :]).astype(BF)
        for p in range(4):
            sorted_ref[p, b * 64 : (b + 1) * 64, :] = part[p * 64 : (p + 1) * 64, :]


def turn_kernel(w_ref, wo_ref, halves_ref, turned_ref):
    half = halves_ref.shape[2]
    halves_ref[0] = w_ref[:, :half]
    halves_ref[1] = w_ref[:, half:]

    @pl.when(pl.program_id(0) == 0)
    def _():
        turned_ref[...] = wo_ref[...].T


def turn_weights(w, wo):
    cols, width = w.shape
    local = wo.shape[0]
    return pl.pallas_call(
        turn_kernel,
        grid=(3,),
        in_specs=[pl.BlockSpec((cols // 3, width), lambda j: (j, 0)), pl.BlockSpec(wo.shape, lambda j: (0, 0))],
        out_specs=[
            pl.BlockSpec((2, cols // 3, width // 2), lambda j: (0, j, 0)),
            pl.BlockSpec((width, local), lambda j: (0, 0)),
        ],
        out_shape=[jax.ShapeDtypeStruct((2, cols, width // 2), BF), jax.ShapeDtypeStruct((width, local), BF)],
        compiler_params=params(56),
        cost_estimate=pl.CostEstimate(flops=0, bytes_accessed=16 * 10**6, transcendentals=0),
        name="turn_weights",
    )(w, wo)


def spread(from_ref, to_ref, rows, offset):
    for core in range(2):
        for place in range(32):
            device = 2 * place + core
            to_ref[(core * 32 + place) * 24 + offset : (core * 32 + place) * 24 + offset + rows, :] = from_ref[
                device * rows : (device + 1) * rows, :
            ]


def forward_kernel(
    x_ref, w_ref, xt_ref, qkv_ref, prob_ref, attn_ref, sorted_ref, heads_ref, turned_ref, wide_ref, part_ref, low_ref, high_ref
):
    heads = qkv_ref.shape[1] // 3
    local = heads * HEAD_DIM
    scale = HEAD_DIM ** -0.5
    p = pl.program_id(0)

    @pl.when(p == 0)
    def _():
        by_patch(x_ref, sorted_ref)
        wide_ref[...] = jnp.zeros_like(wide_ref)

    xt = sorted_ref[p].T
    for j in range(3):
        part = mm(w_ref[j * local : (j + 1) * local, :], xt)
        qkv_ref[0, j * heads : (j + 1) * heads] = part.reshape(heads, HEAD_DIM, 256).astype(BF)
    turned_ref[...] = x_ref[pl.ds(pl.multiple_of(p * 256, 256), 256), :].T.astype(F32)
    spread(turned_ref, wide_ref, 22, 0)
    xt_ref[...] = wide_ref[...].astype(BF).reshape(xt_ref.shape)
    for h in range(heads):
        query = qkv_ref[0, h]
        key = qkv_ref[0, heads + h]
        value = qkv_ref[0, 2 * heads + h]
        scores = mm(key.T, query) * scale
        expo = jnp.exp(scores - jnp.max(scores, axis=0, keepdims=True))
        prob = expo / jnp.sum(expo, axis=0, keepdims=True)
        prob_ref[0, h] = prob
        heads_ref[p, h * HEAD_DIM : (h + 1) * HEAD_DIM, :] = mm(value, prob.astype(BF))

    @pl.when(p == 3)
    def _():
        low_ref[...] = jnp.zeros_like(low_ref)
        high_ref[...] = jnp.zeros_like(high_ref)
        perm = onehot(
            512,
            512,
            lambda r, c: ((r >> 7) == ((c >> 2) & 3)) & (((r >> 2) & 31) == (c >> 4)) & ((r & 3) == (c & 3)),
        )
        for b in range(2):
            cols = jnp.concatenate([heads_ref[q, :, b * 128 : (b + 1) * 128] for q in range(4)], axis=1)
            part_ref[...] = mm(cols.astype(BF), perm)
            spread(part_ref, low_ref, 11, 0)
            spread(part_ref, high_ref, 11, 11)
            rows = attn_ref.shape[1]
            attn_ref[:, :, b * 512 : (b + 1) * 512] = low_ref[...].astype(BF).reshape(2, rows, 512)
            attn_ref[:, :, 1024 + b * 512 : 1024 + (b + 1) * 512] = high_ref[...].astype(BF).reshape(2, rows, 512)


def forward(x, w):
    tokens, width = x.shape
    heads = w.shape[0] // 3 // HEAD_DIM
    local = heads * HEAD_DIM
    once = pl.Buffered(buffer_count=1)
    return pl.pallas_call(
        forward_kernel,
        grid=(4,),
        in_specs=[
            pl.BlockSpec((tokens, width), lambda p: (0, 0), pipeline_mode=once),
            pl.BlockSpec(w.shape, lambda p: (0, 0), pipeline_mode=once),
        ],
        out_specs=[
            pl.BlockSpec((2, 768, 256), lambda p: (0, 0, p)),
            pl.BlockSpec((1, 3 * heads, HEAD_DIM, 256), lambda p: (p, 0, 0, 0)),
            pl.BlockSpec((1, heads, 256, 256), lambda p: (p, 0, 0, 0)),
            pl.BlockSpec((2, 768, 2 * tokens), lambda p: (0, 0, 0)),
        ],
        out_shape=[
            jax.ShapeDtypeStruct((2, 768, tokens), BF),
            jax.ShapeDtypeStruct((4, 3 * heads, HEAD_DIM, 256), BF),
            jax.ShapeDtypeStruct((4, heads, 256, 256), F32),
            jax.ShapeDtypeStruct((2, 768, 2 * tokens), BF),
        ],
        scratch_shapes=[
            pltpu.VMEM((4, 256, width), BF),
            pltpu.VMEM((4, local, 256), F32),
            pltpu.VMEM((width, 256), F32),
            pltpu.VMEM((1536, 256), F32),
            pltpu.VMEM((local, 512), F32),
            pltpu.VMEM((1536, 512), F32),
            pltpu.VMEM((1536, 512), F32),
        ],
        compiler_params=params(60),
        cost_estimate=pl.CostEstimate(flops=9 * 10**9, bytes_accessed=24 * 10**6, transcendentals=4 * heads * 65536),
        name="forward",
    )(x, w)


def backward_kernel(
    c_ref, wo_ref, w_any, qkv_ref, prob_ref, dqkv_ref, send_ref, sorted_ref, grad_ref, terms_ref, patch_ref, w_ref, sem
):
    heads = prob_ref.shape[1]
    local = heads * HEAD_DIM
    scale = HEAD_DIM ** -0.5
    p = pl.program_id(0)
    weights = pltpu.make_async_copy(w_any, w_ref, sem)

    @pl.when(p == 0)
    def _():
        weights.start()
        terms_ref[...] = mm(c_ref[...], wo_ref[...])
        perm = onehot(
            256,
            256,
            lambda r, c: ((r >> 6) == ((c >> 2) & 3)) & (((r >> 2) & 15) == (c >> 4)) & ((r & 3) == (c & 3)),
        )
        for b in range(4):
            part = mm(perm, terms_ref[b * 256 : (b + 1) * 256, :].astype(BF)).astype(BF)
            for q in range(4):
                sorted_ref[q, b * 64 : (b + 1) * 64, :] = part[q * 64 : (q + 1) * 64, :]

    grad_ref[...] = sorted_ref[p].T.astype(F32).reshape(heads, HEAD_DIM, 256).astype(BF)
    for h in range(heads):
        query = qkv_ref[0, h]
        key = qkv_ref[0, heads + h]
        value = qkv_ref[0, 2 * heads + h]
        gout = grad_ref[h]
        prob = prob_ref[0, h]
        dvalue = mm(gout, prob.astype(BF), NT)
        dweights = mm(value.T, gout)
        mean = jnp.sum(prob * dweights, axis=0, keepdims=True)
        dscores = (prob * (dweights - mean) * scale).astype(BF)
        dquery = mm(key, dscores)
        dkey = mm(query, dscores, NT)
        for j, value in enumerate((dquery, dkey, dvalue)):
            at = j * local + h * HEAD_DIM
            patch_ref[p, at : at + HEAD_DIM, :] = value

    @pl.when(p == 3)
    def _():
        weights.wait()
        perm = onehot(
            256,
            256,
            lambda r, c: ((c >> 6) == ((r >> 2) & 3)) & (((c >> 2) & 15) == (r >> 4)) & ((r & 3) == (c & 3)),
        )
        turned = [patch_ref[q].astype(BF).T for q in range(4)]
        for b in range(4):
            rows = jnp.concatenate([turned[q][b * 64 : (b + 1) * 64, :] for q in range(4)], axis=0)
            dqkv_ref[b * 256 : (b + 1) * 256, :] = mm(perm, rows).astype(BF)
        for t in range(2):
            terms_ref[...] = mm(dqkv_ref[...], w_ref[t])
            send_ref[:, t] = terms_ref[...].astype(BF).reshape(64, 16, terms_ref.shape[1])


def backward(cot, wo, w, qkv, prob):
    tokens, width = cot.shape
    heads = prob.shape[1]
    local = heads * HEAD_DIM
    once = pl.Buffered(buffer_count=1)
    return pl.pallas_call(
        backward_kernel,
        grid=(4,),
        in_specs=[
            pl.BlockSpec((tokens, width), lambda p: (0, 0), pipeline_mode=once),
            pl.BlockSpec(wo.shape, lambda p: (0, 0), pipeline_mode=once),
            pl.BlockSpec(memory_space=pl.ANY),
            pl.BlockSpec((1, 3 * heads, HEAD_DIM, 256), lambda p: (p, 0, 0, 0)),
            pl.BlockSpec((1, heads, 256, 256), lambda p: (p, 0, 0, 0)),
        ],
        out_specs=[
            pl.BlockSpec((tokens, 3 * local), lambda p: (0, 0)),
            pl.BlockSpec((64, 2, 16, width // 2), lambda p: (0, 0, 0, 0)),
        ],
        out_shape=[
            jax.ShapeDtypeStruct((tokens, 3 * local), BF),
            jax.ShapeDtypeStruct((64, 2, 16, width // 2), BF),
        ],
        scratch_shapes=[
            pltpu.VMEM((4, 256, local), BF),
            pltpu.VMEM((heads, HEAD_DIM, 256), BF),
            pltpu.VMEM((tokens, local), F32),
            pltpu.VMEM((4, 3 * local, 256), F32),
            pltpu.VMEM(w.shape, BF),
            pltpu.SemaphoreType.DMA,
        ],
        compiler_params=params(60),
        cost_estimate=pl.CostEstimate(flops=12 * 10**9, bytes_accessed=30 * 10**6, transcendentals=0),
        name="backward",
    )(cot, wo, w, qkv, prob)


def weights_kernel(core_ref, xt_ref, dqkv_ref, attn_ref, c_ref, o_ref, halves_ref):
    tokens, cols = dqkv_ref.shape
    half = c_ref.shape[1] // 2
    places = o_ref.shape[0]

    @pl.when(pl.program_id(0) == 0)
    def _():
        halves_ref[:tokens] = c_ref[:, :half]
        halves_ref[tokens:] = c_ref[:, half:]

    o_ref[:, :, :cols] = mm(xt_ref[0], dqkv_ref[...]).astype(BF).reshape(places, 24, cols)
    o_ref[:, :, cols:] = mm(attn_ref[0], halves_ref[...]).astype(BF).reshape(places, 24, half)


def weight_grads(core, xt, dqkv, attn, cot):
    tokens, cols = dqkv.shape
    half = cot.shape[1] // 2
    once = pl.Buffered(buffer_count=1)
    return pl.pallas_call(
        weights_kernel,
        grid_spec=pltpu.PrefetchScalarGridSpec(
            num_scalar_prefetch=1,
            grid=(2,),
            in_specs=[
                pl.BlockSpec((1, 384, tokens), lambda s, core: (core[0], s, 0)),
                pl.BlockSpec(dqkv.shape, lambda s, core: (0, 0), pipeline_mode=once),
                pl.BlockSpec((1, 384, 2 * tokens), lambda s, core: (core[0], s, 0)),
                pl.BlockSpec(cot.shape, lambda s, core: (0, 0), pipeline_mode=once),
            ],
            out_specs=pl.BlockSpec((16, 24, cols + half), lambda s, core: (s, 0, 0)),
            scratch_shapes=[pltpu.VMEM((2 * tokens, half), BF)],
        ),
        out_shape=jax.ShapeDtypeStruct((32, 24, cols + half), BF),
        compiler_params=params(56),
        cost_estimate=pl.CostEstimate(flops=6 * 10**9, bytes_accessed=18 * 10**6, transcendentals=0),
        name="weight_grads",
    )(core, xt, dqkv, attn, cot)


def split_kernel(at_ref, *refs, n_terms):
    k = pl.program_id(0)
    low, high, outs = refs[:n_terms], refs[n_terms : 2 * n_terms], refs[2 * n_terms :]
    for group, terms in ((0, low), (1, high)):
        total = terms[0][...].astype(F32)
        for term in terms[1:]:
            total += term[...].astype(F32)
        for q in range(4):

            @pl.when(k == q)
            def _():
                outs[4 * group + q][...] = total.astype(BF).reshape(outs[q].shape)


def split_sum(at, lows, highs, low_spec, high_spec, shape, name):
    n_terms = len(lows)
    whole = pl.BlockSpec(shape, lambda k, at: (0,) * len(shape))
    return pl.pallas_call(
        functools.partial(split_kernel, n_terms=n_terms),
        grid_spec=pltpu.PrefetchScalarGridSpec(
            num_scalar_prefetch=1,
            grid=(4,),
            in_specs=[low_spec] * n_terms + [high_spec] * n_terms,
            out_specs=[whole] * 8,
        ),
        out_shape=[jax.ShapeDtypeStruct(shape, BF)] * 8,
        compiler_params=params(40),
        cost_estimate=pl.CostEstimate(flops=10**6, bytes_accessed=10 * shape[0] * shape[-1] * 24, transcendentals=0),
        name=name,
    )(at, *lows, *highs)


def pair_kernel(at_ref, *refs):
    mine_ref, other_ref = refs[8:]
    for group in range(2):
        total = refs[4 * group][...].astype(F32)
        for term in refs[4 * group + 1 : 4 * group + 4]:
            total += term[...].astype(F32)
        z = at_ref[2]
        mine_ref[group] = jnp.where(z == 0, total[0], total[1])
        other_ref[group] = jnp.where(z == 0, total[1], total[0]).astype(BF)


def pair_sum(at, terms):
    shape = terms[0].shape
    return pl.pallas_call(
        pair_kernel,
        in_specs=[pl.BlockSpec(memory_space=pltpu.SMEM)] + [pl.BlockSpec(memory_space=pltpu.VMEM)] * 8,
        out_shape=[jax.ShapeDtypeStruct(shape, F32), jax.ShapeDtypeStruct(shape, BF)],
        compiler_params=params(16),
        name="pair_sum",
    )(at, *terms)


def final_kernel(mine_ref, other_ref, qkv_ref, out_ref):
    half = out_ref.shape[1] // 2
    low = mine_ref[0] + other_ref[0].astype(F32)
    high = mine_ref[1] + other_ref[1].astype(F32)
    qkv_ref[0] = low[:22, :half]
    qkv_ref[1] = low[:22, half:]
    qkv_ref[2] = high[:22, :half]
    out_ref[:, :half] = high[:11, half:]
    out_ref[:, half:] = high[11:22, half:]


def final_sum(mine, other):
    width = mine.shape[2]
    return pl.pallas_call(
        final_kernel,
        out_shape=[jax.ShapeDtypeStruct((3, 22, width // 2), F32), jax.ShapeDtypeStruct((11, width), F32)],
        compiler_params=params(16),
        name="final_sum",
    )(mine, other)


def sum_over_chips(mine, arrived, at):
    width = mine.shape[1] // 2
    mine, arrived = (a.reshape(2, 4, 4, 24, 2 * width) for a in (mine, arrived))

    def to(step_x, step_y, flip=0):
        pairs = []
        for i in range(64):
            z, x, y, core = i // 32, i // 8 % 4, i // 2 % 4, i % 2
            pairs.append((i, (((z ^ flip) * 4 + (x + step_x) % 4) * 4 + (y + step_y) % 4) * 2 + core))
        return pairs

    first = split_sum(
        at,
        [mine, arrived],
        [mine, arrived],
        pl.BlockSpec((2, 1, 4, 24, width), lambda k, at: (0, (at[0] + k) % 4, 0, 0, 0)),
        pl.BlockSpec((2, 4, 1, 24, width), lambda k, at: (0, 0, (at[1] + k) % 4, 0, 1)),
        (2, 4, 24, width),
        "core_sum",
    )
    lows = [first[0]] + [lax.ppermute(first[k], "seq", to(k, 0)) for k in (1, 2, 3)]
    highs = [first[4]] + [lax.ppermute(first[4 + k], "seq", to(0, k)) for k in (1, 2, 3)]
    second = split_sum(
        at,
        lows,
        highs,
        pl.BlockSpec((2, 1, 24, width), lambda k, at: (0, (at[1] + k) % 4, 0, 0)),
        pl.BlockSpec((2, 1, 24, width), lambda k, at: (0, (at[0] + k) % 4, 0, 0)),
        (2, 24, width),
        "ring_sum",
    )
    lows = [second[0]] + [lax.ppermute(second[k], "seq", to(0, k)) for k in (1, 2, 3)]
    highs = [second[4]] + [lax.ppermute(second[4 + k], "seq", to(k, 0)) for k in (1, 2, 3)]
    kept, given = pair_sum(at, lows + highs)
    return final_sum(kept, lax.ppermute(given, "seq", to(0, 0, 1)))


def unpack_kernel(x_ref, o_ref):
    half = x_ref.shape[2]
    pick = onehot(
        1024,
        512,
        lambda r, c: ((r & 3) == (c >> 7)) & ((r >> 5) == ((c >> 2) & 31)) & (((r >> 2) & 3) == (c & 3)),
    )
    for b in range(2):
        rows = x_ref[b * 64 : (b + 1) * 64].reshape(1024, half)
        part = mm(rows.T, pick).astype(BF)
        for f in range(4):
            o_ref[:, f * 256 + b * 128 : f * 256 + (b + 1) * 128] = part[:, f * 128 : (f + 1) * 128]


def unpack(x):
    half = x.shape[2]
    return pl.pallas_call(
        unpack_kernel,
        out_shape=jax.ShapeDtypeStruct((half, 1024), BF),
        compiler_params=params(32),
        cost_estimate=pl.CostEstimate(flops=2 * half * 1024 * 1024, bytes_accessed=5 * 10**6, transcendentals=0),
        name="unpack_rows",
    )(x)


def shards(hidden, out_cotangent, qkv_weight, out_weight):
    tokens, width = hidden.shape
    local = qkv_weight.shape[2]
    n_seq = lax.axis_size("seq")
    w_rows = qkv_weight.transpose(1, 2, 0).reshape(3 * local, width)
    w_halves, wo_turned = turn_weights(w_rows, out_weight)

    def to_patches(rows):
        return lax.all_to_all(rows.reshape(n_seq, 16, width), "seq", split_axis=0, concat_axis=0, tiled=True).reshape(tokens, width)

    hidden_in = to_patches(pack(hidden))
    cot_send = pack(out_cotangent)
    hidden_in, cot_send, w_halves, wo_turned = lax.optimization_barrier((hidden_in, cot_send, w_halves, wo_turned))
    cot_in = to_patches(cot_send)
    xt, qkv, prob, attn = forward(hidden_in, w_rows)
    dqkv, send = backward(cot_in, wo_turned, w_halves, qkv, prob)

    returned = lax.all_to_all(send.reshape(2 * n_seq, 16, width // 2), ("seq", "tp"), split_axis=0, concat_axis=0, tiled=True)
    place = lax.axis_index("seq").astype(jnp.int32)
    core = place % 2
    at = jnp.stack([place // 8 % 4, place // 2 % 4, place // 32])
    grads = functools.partial(weight_grads, xt=xt, dqkv=dqkv, attn=attn, cot=cot_in)
    other = grads((1 - core).reshape(1))
    arrived = lax.ppermute(other, "seq", [(i, i ^ 1) for i in range(n_seq)])
    mine = grads(core.reshape(1))
    shape = (32 * 24, 3 * local + width // 2)
    qkv_grad, out_grad = sum_over_chips(mine.reshape(shape), arrived.reshape(shape), at)
    return (unpack(returned).T, qkv_grad.transpose(1, 0, 2), out_grad)


def solution(mesh):
    return jax.shard_map(
        shards,
        mesh=mesh,
        in_specs=(P("seq", None), P("seq", None), P(None, None, "tp"), P("tp", None)),
        out_specs=(P("seq", "tp"), P("seq", None, "tp"), P(("tp", "seq"), None)),
        check_vma=False,
    )
```

time: 278 us -> 243 us (0.87)
  waiting for transfers between devices: 104 us -> 68.9 us
  starting transfers between devices: 34.5 us -> 52.4 us
  local copies, waits for them, and re-layouts: 17.1 us -> 5.56 us
  other arithmetic: 9.52 us -> 0.08 us
  Pallas kernels: 109 us -> 112 us
    all_to_all x1 -> x0, waiting for transfers between devices: 56.9 us -> none  [shards(): lax.all_to_all(chip, 'seq', split_axis=0, concat_axis=0, tiled=True, axis...]
    ppermute x0 -> x13, waiting for transfers between devices: none -> 35.8 us  [the longest x3 27.5 us: sum_over_chips(): lax.ppermute(first[k], 'seq', to(k, 0))]
    ppermute x0 -> x13, starting transfers between devices: none -> 24.1 us  [the longest x3 7.19 us: sum_over_chips(): lax.ppermute(first[4 + k], 'seq', to(0, k))]
    all_to_all x1, waiting for transfers between devices: 13.1 us -> 0.01 us  [shards(): lax.all_to_all(send.reshape(2 * n_seq, 16, width // 2), ('seq', 'tp'), sp...]
    optimization_barrier x1 -> x0, local copies, waits for them, and re-layouts: 8.93 us -> none  [shards(): lax.optimization_barrier((hidden_in, cot_send, w_cols))]
    convert_element_type x1 -> x0, other arithmetic: 6.61 us -> none  [shards(): chip = (mine.astype(F32) + arrived.astype(F32)).astype(BF)]
    all_to_all x1 -> x0, starting transfers between devices: 6.05 us -> none  [shards(): lax.all_to_all(chip, 'seq', split_axis=0, concat_axis=0, tiled=True, axis...]
    pallas_call x1, Pallas kernels: 24.5 us -> 29 us  [forward(): pl.pallas_call(forward_kernel, grid=(4,), in_specs=[pl.BlockSpec((tokens,...]
  transfers between devices with their start and end apart: 5 -> 17, of which waited for: 4 -> 11; matrix products, arithmetic and copies ran while one was open for 7% -> 0% of each run, Pallas kernels for 19% -> 27%
where the time goes in v2:
time: 243 us; the launch traced here: 239 us
  Pallas kernels  112 us (46%)
  waiting for transfers between devices  68.9 us (28%)
  starting transfers between devices  52.4 us (22%)
  local copies, waits for them, and re-layouts  5.56 us (2%)
    all_to_all x2, waiting for transfers between devices, to_patches(): lax.all_to_all(rows.reshape(n_seq, 16, width), 'seq', split_axis=0, conca...  33.1 us
    pallas_call x1, Pallas kernels, backward(): pl.pallas_call(backward_kernel, grid=(4,), in_specs=[pl.BlockSpec((tokens...  30.1 us
    pallas_call x1, Pallas kernels, forward(): pl.pallas_call(forward_kernel, grid=(4,), in_specs=[pl.BlockSpec((tokens,...  29 us
    ppermute x3, waiting for transfers between devices, sum_over_chips(): lax.ppermute(first[k], 'seq', to(k, 0))  27.5 us
    pallas_call x2, Pallas kernels, weight_grads(): pl.pallas_call(weights_kernel, grid_spec=pltpu.PrefetchScalarGridSpec(num...  25 us
    all_to_all x2, starting transfers between devices, to_patches(): lax.all_to_all(rows.reshape(n_seq, 16, width), 'seq', split_axis=0, conca...  17.6 us
    all_to_all x1, starting transfers between devices, shards(): lax.all_to_all(send.reshape(2 * n_seq, 16, width // 2), ('seq', 'tp'), sp...  10.5 us
    pallas_call x1, Pallas kernels, turn_weights(): pl.pallas_call(turn_kernel, grid=(3,), in_specs=[pl.BlockSpec((cols // 3,...  8.8 us
  transfers between devices with their start and end apart: 17, of which 11 were waited for; matrix products, arithmetic and copies ran while one was open for 0% of the time, Pallas kernels for 27%

profile of v2, /device:TPU:32, one launch (start us, length us, event | category | flops | bytes accessed | tf_op | source)
XLA Modules:
  0.0 239.2 jit_solution(14955536394141455813)
XLA Ops:
  0.6 0.0 copy-start.1
  0.6 1.8 copy-done.1
  2.4 3.1 %pack_rows.2 = bf16[1024,1408]{1,0:T(8,128)(2,1)} custom-call(bf16[4,256,1408]{2,1,0:T(8,128)(2,1)S(1)} %bitcast.21), custom_call_target="tpu_custom_call" | custom-call | flops 738197504 | bytes 5767168 | tf_op jit(solution)/shard_map/pack_rows/pallas_call | solution.py:46
  5.6 9.2 %all-to-all-start = ((bf16[64,16,1408]{2,1,0:T(8,128)(2,1)}), bf16[64,16,1408]{2,1,0:T(8,128)(2,1)}, u32[]{:S(2)}, u32[]{:S(2)}) async-start(bf16[64,16,1408]{2,1,0:T(8,128)(2,1)} %bitcast.1), calls=%async_computation | async-start | bytes 5767168 | tf_op jit(solution)/shard_map/all_to_all | solution.py:473
  14.8 0.0 copy-start.2
  14.8 8.8 %turn_weights.1 = (bf16[2,2112,704]{2,1,0:T(8,128)(2,1)}, bf16[1408,704]{1,0:T(8,128)(2,1)}) custom-call(bf16[2112,1408]{1,0:T(8,128)(2,1)} %bitcast.23, bf16[704,1408]{1,0:T(8,128)(2,1)} %wo_ref.1), custom_call_target="tpu_custom_call" | custom-call | bytes 16000000 | tf_op jit(solution)/shard_map/turn_weights/pallas_call | solution.py:83
  23.6 0.0 copy-done.2
  23.6 3.1 %pack_rows.3 = bf16[1024,1408]{1,0:T(8,128)(2,1)} custom-call(bf16[4,256,1408]{2,1,0:T(8,128)(2,1)S(1)} %bitcast.22), custom_call_target="tpu_custom_call" | custom-call | flops 738197504 | bytes 5767168 | tf_op jit(solution)/shard_map/pack_rows/pallas_call | solution.py:46
  26.7 25.1 %all-to-all-done = bf16[64,16,1408]{2,1,0:T(8,128)(2,1)} async-done(((bf16[64,16,1408]{2,1,0:T(8,128)(2,1)}), bf16[64,16,1408]{2,1,0:T(8,128)(2,1)}, u32[]{:S(2)}, u32[]{:S(2)}) %all-to-all-start) | async-done | bytes 2883616 | tf_op jit(solution)/shard_map/all_to_all | solution.py:473
  51.8 8.4 %all-to-all-start.1 = ((bf16[64,16,1408]{2,1,0:T(8,128)(2,1)}), bf16[64,16,1408]{2,1,0:T(8,128)(2,1)S(1)}, u32[]{:S(2)}, u32[]{:S(2)}) async-start(bf16[64,16,1408]{2,1,0:T(8,128)(2,1)} %bitcast.6), calls=%async_computation.1 | async-start | bytes 5767168 | tf_op jit(solution)/shard_map/all_to_all | solution.py:473
  60.3 29.0 %forward.1 = (bf16[2,768,1024]{2,1,0:T(8,128)(2,1)}, bf16[4,24,88,256]{3,2,1,0:T(8,128)(2,1)}, f32[4,8,256,256]{3,2,1,0:T(8,128)}, bf16[2,768,2048]{2,1,0:T(8,128)(2,1)}) custom-call(bf16[1024,1408]{1,0:T(8,128)(2,1)} %bitcast.2.x_ref, bf16[2112,1408]{1,0:T(8,128)(2,1)} %bitcast.24), custom_call_target="tpu_custom_call" | custom-call | flops 8999999488 | bytes 24000000 | tf_op jit(solution)/shard_map/forward/pallas_call | solution.py:161
  89.3 8.0 %all-to-all-done.1 = bf16[64,16,1408]{2,1,0:T(8,128)(2,1)S(1)} async-done(((bf16[64,16,1408]{2,1,0:T(8,128)(2,1)}), bf16[64,16,1408]{2,1,0:T(8,128)(2,1)S(1)}, u32[]{:S(2)}, u32[]{:S(2)}) %all-to-all-start.1) | async-done | bytes 2883616 | tf_op jit(solution)/shard_map/all_to_all | solution.py:473
  97.3 0.0 copy-start.3
  97.3 1.5 copy-done.3
  98.8 30.1 %backward.1 = (bf16[1024,2112]{1,0:T(8,128)(2,1)}, bf16[64,2,16,704]{3,2,1,0:T(8,128)(2,1)}) custom-call(bf16[1024,1408]{1,0:T(8,128)(2,1)} %bitcast.26, bf16[1408,704]{1,0:T(8,128)(2,1)} %get-tuple-element.38.wo_ref, bf16[2,2112,704]{2,1,0:T(8,128)(2,1)} %get-tuple-element.39.w_any, bf16[4,24,88,256]{3,2,1,0:T(8,128)(2,1)} %get-tuple-element.41.qkv_ref, ...), custom_call_target="tpu_custom_call" | custom-call | flops 12000000000 | bytes 30000000 | tf_op jit(solution)/shard_map/backward/pallas_call | solution.py:257
  129.0 12.6 %weight_grads.3 = bf16[32,24,2816]{2,1,0:T(8,128)(2,1)} custom-call(s32[1]{0:T(128)} %bitcast.16.core_ref, bf16[2,768,1024]{2,1,0:T(8,128)(2,1)} %get-tuple-element.44.xt_ref, bf16[1024,2112]{1,0:T(8,128)(2,1)} %get-tuple-element.45.dqkv_ref, bf16[2,768,2048]{2,1,0:T(8,128)(2,1)} %get-tuple-element.46.attn_ref, bf16[1024,1408]{1,0:T(8,128)(2,1)} %bitcast.27), custom_call_target="tpu_custom_call" | custom-call | flops 6000000000 | bytes 18000000 | tf_op jit(solution)/shard_map/weight_grads/pallas_call | solution.py:307
  141.6 0.1 collective-permute-start
  141.7 10.5 %all-to-all-start.2 = ((bf16[128,16,704]{2,1,0:T(8,128)(2,1)}), bf16[128,16,704]{2,1,0:T(8,128)(2,1)S(1)}, u32[]{:S(2)}, u32[]{:S(2)}) async-start(bf16[128,16,704]{2,1,0:T(8,128)(2,1)} %bitcast.25), calls=%async_computation.2 | async-start | bytes 6291456 | tf_op jit(solution)/shard_map/all_to_all | solution.py:482
  152.2 0.1 pad_add_fusion.at_ref
  152.3 12.4 %weight_grads.2 = bf16[32,24,2816]{2,1,0:T(8,128)(2,1)} custom-call(s32[1]{0:T(128)} %bitcast.14.core_ref, bf16[2,768,1024]{2,1,0:T(8,128)(2,1)} %get-tuple-element.44.xt_ref, bf16[1024,2112]{1,0:T(8,128)(2,1)} %get-tuple-element.45.dqkv_ref, bf16[2,768,2048]{2,1,0:T(8,128)(2,1)} %get-tuple-element.46.attn_ref, bf16[1024,1408]{1,0:T(8,128)(2,1)} %bitcast.28), custom_call_target="tpu_custom_call" | custom-call | flops 6000000000 | bytes 18000000 | tf_op jit(solution)/shard_map/weight_grads/pallas_call | solution.py:307
  164.7 0.0 collective-permute-done
  164.7 0.0 copy-start
  164.7 2.2 copy-done
  166.9 5.0 %core_sum.1 = (bf16[2,4,24,1408]{3,2,1,0:T(8,128)(2,1)S(1)}, bf16[2,4,24,1408]{3,2,1,0:T(8,128)(2,1)S(1)}, bf16[2,4,24,1408]{3,2,1,0:T(8,128)(2,1)S(1)}, bf16[2,...) custom-call(s32[3]{0:T(128)S(1)} %pad_add_fusion.at_ref, ...), custom_call_target="tpu_custom_call" | custom-call | flops 1000000 | bytes 675840 | tf_op jit(solution)/shard_map/core_sum/pallas_call | solution.py:345
  171.9 1.6 collective-permute-start.1
  173.5 2.7 %collective-permute-start.2 = (bf16[2,4,24,1408]{3,2,1,0:T(8,128)(2,1)S(1)}, bf16[2,4,24,1408]{3,2,1,0:T(8,128)(2,1)S(1)}, u32[]{:S(2)}, u32[]{:S(2)}) collective-permute-start(bf16[2,4,24,1408]{3,2,1,0:T(8,128)(2,1)S(1)} %get-tuple-element.49), channel_id=1, source_target_pairs={{0,32},{2,34},{4,36},{6,38},{8,40},{10,42},{12,44},{14,46},{16,48}... | collective-permute-start | bytes 1622024 | tf_op jit(solution)/shard_map/ppermute | solution.py:423
  176.2 1.4 collective-permute-start.3
  177.7 1.5 collective-permute-start.4
  179.2 2.8 %collective-permute-start.5 = (bf16[2,4,24,1408]{3,2,1,0:T(8,128)(2,1)S(1)}, bf16[2,4,24,1408]{3,2,1,0:T(8,128)(2,1)S(1)}, u32[]{:S(2)}, u32[]{:S(2)}) collective-permute-start(bf16[2,4,24,1408]{3,2,1,0:T(8,128)(2,1)S(1)} %get-tuple-element.53), channel_id=1, source_target_pairs={{0,8},{2,10},{4,12},{6,14},{8,0},{10,2},{12,4},{14,6},{16,24},{18,... | collective-permute-start | bytes 1622024 | tf_op jit(solution)/shard_map/ppermute | solution.py:424
  182.0 18.7 %collective-permute-done.1.refs_1_ = bf16[2,4,24,1408]{3,2,1,0:T(8,128)(2,1)S(1)} collective-permute-done((bf16[2,4,24,1408]{3,2,1,0:T(8,128)(2,1)S(1)}, bf16[2,4,24,1408]{3,2,1,0:T(8,128)(2,1)S(1)}, u32[]{:S(2)}, u32[]{:S(2)}) %collective-permute-start.1) | collective-permute-done | bytes 540704 | tf_op jit(solution)/shard_map/ppermute | solution.py:423
  200.7 2.9 %collective-permute-start.6 = (bf16[2,4,24,1408]{3,2,1,0:T(8,128)(2,1)S(1)}, bf16[2,4,24,1408]{3,2,1,0:T(8,128)(2,1)S(1)}, u32[]{:S(2)}, u32[]{:S(2)}) collective-permute-start(bf16[2,4,24,1408]{3,2,1,0:T(8,128)(2,1)S(1)} %get-tuple-element.54), channel_id=1, source_target_pairs={{0,12},{2,14},{4,0},{6,2},{8,4},{10,6},{12,8},{14,10},{16,28},{18,... | collective-permute-start | bytes 1622024 | tf_op jit(solution)/shard_map/ppermute | solution.py:424
  203.6 8.8 %collective-permute-done.2.refs_2_ = bf16[2,4,24,1408]{3,2,1,0:T(8,128)(2,1)S(1)} collective-permute-done((bf16[2,4,24,1408]{3,2,1,0:T(8,128)(2,1)S(1)}, bf16[2,4,24,1408]{3,2,1,0:T(8,128)(2,1)S(1)}, u32[]{:S(2)}, u32[]{:S(2)}) %collective-permute-start.2) | collective-permute-done | bytes 540704 | tf_op jit(solution)/shard_map/ppermute | solution.py:423
  212.4 0.0 collective-permute-done.3.refs_3_
  212.4 0.0 collective-permute-done.4.refs_5_
  212.4 1.1 collective-permute-done.5.refs_6_
  213.5 1.4 collective-permute-done.6.refs_7_
  214.9 2.3 ring_sum.1
  217.2 1.2 collective-permute-start.7
  218.4 4.0 %collective-permute-start.8 = (bf16[2,24,1408]{2,1,0:T(8,128)(2,1)S(1)}, bf16[2,24,1408]{2,1,0:T(8,128)(2,1)S(1)}, u32[]{:S(2)}, u32[]{:S(2)}) collective-permute-start(bf16[2,24,1408]{2,1,0:T(8,128)(2,1)S(1)} %get-tuple-element.57), channel_id=1, source_target_pairs={{0,8},{2,10},{4,12},{6,14},{8,0},{10,2},{12,4},{14,6},{16,24},{18,... | collective-permute-start | bytes 405512 | tf_op jit(solution)/shard_map/ppermute | solution.py:434
  222.5 0.2 collective-permute-start.9
  222.6 0.0 collective-permute-start.10
  222.6 2.2 collective-permute-start.11
  224.8 0.6 collective-permute-done.7.refs_1_
  225.4 0.9 collective-permute-start.12
  226.3 1.2 collective-permute-done.8.refs_2_
  227.5 0.0 collective-permute-done.9.refs_3_
  227.5 2.8 %collective-permute-done.10.refs_5_ = bf16[2,24,1408]{2,1,0:T(8,128)(2,1)S(1)} collective-permute-done((bf16[2,24,1408]{2,1,0:T(8,128)(2,1)S(1)}, bf16[2,24,1408]{2,1,0:T(8,128)(2,1)S(1)}, u32[]{:S(2)}, u32[]{:S(2)}) %collective-permute-start.10) | collective-permute-done | bytes 135200 | tf_op jit(solution)/shard_map/ppermute | solution.py:435
  230.3 0.0 collective-permute-done.11.refs_6_
  230.3 0.9 collective-permute-done.12.refs_7_
  231.2 1.3 pair_sum.1
  232.5 2.7 %collective-permute-start.13 = (bf16[2,24,1408]{2,1,0:T(8,128)(2,1)}, bf16[2,24,1408]{2,1,0:T(8,128)(2,1)S(1)}, u32[]{:S(2)}, u32[]{:S(2)}) collective-permute-start(bf16[2,24,1408]{2,1,0:T(8,128)(2,1)} %get-tuple-element.64), channel_id=1, source_target_pairs={{0,64},{2,66},{4,68},{6,70},{8,72},{10,74},{12,76},{14,78},{16,80}... | collective-permute-start | bytes 405512 | tf_op jit(solution)/shard_map/ppermute | solution.py:437
  235.2 0.0 all-to-all-done.2.x_ref
  235.2 2.9 %unpack_rows.1 = bf16[704,1024]{1,0:T(8,128)(2,1)} custom-call(bf16[128,16,704]{2,1,0:T(8,128)(2,1)S(1)} %all-to-all-done.2.x_ref), custom_call_target="tpu_custom_call" | custom-call | flops 1476395008 | bytes 5000000 | tf_op jit(solution)/shard_map/unpack_rows/pallas_call | solution.py:456
  238.1 0.3 collective-permute-done.13.other_ref
  238.4 0.8 final_sum.1
Async XLA Ops:
  0.6 1.8 copy-start.1
  5.6 46.2 %all-to-all-start = ((bf16[64,16,1408]{2,1,0:T(8,128)(2,1)}), bf16[64,16,1408]{2,1,0:T(8,128)(2,1)}, u32[]{:S(2)}, u32[]{:S(2)}) async-start(bf16[64,16,1408]{2,1,0:T(8,128)(2,1)} %bitcast.1), calls=%async_computation | async-start | bytes 5767168 | tf_op jit(solution)/shard_map/all_to_all | solution.py:473
  14.8 8.8 %copy-start.2 = (bf16[1024,1408]{1,0:T(8,128)(2,1)S(1)}, bf16[1024,1408]{1,0:T(8,128)(2,1)}, u32[]{:S(2)}) copy-start(bf16[1024,1408]{1,0:T(8,128)(2,1)} %param.5) | copy-start | bytes 8650756
  51.8 45.5 %all-to-all-start.1 = ((bf16[64,16,1408]{2,1,0:T(8,128)(2,1)}), bf16[64,16,1408]{2,1,0:T(8,128)(2,1)S(1)}, u32[]{:S(2)}, u32[]{:S(2)}) async-start(bf16[64,16,1408]{2,1,0:T(8,128)(2,1)} %bitcast.6), calls=%async_computation.1 | async-start | bytes 5767168 | tf_op jit(solution)/shard_map/all_to_all | solution.py:473
  97.3 1.5 copy-start.3
  141.6 23.1 %collective-permute-start = (bf16[32,24,2816]{2,1,0:T(8,128)(2,1)}, bf16[32,24,2816]{2,1,0:T(8,128)(2,1)}, u32[]{:S(2)}, u32[]{:S(2)}) collective-permute-start(bf16[32,24,2816]{2,1,0:T(8,128)(2,1)} %weight_grads.3), channel_id=1, source_target_pairs={{0,2},{2,0},{4,6},{6,4},{8,10},{10,8},{12,14},{14,12},{16,18},{18,... | collective-permute-start | bytes 12976136 | tf_op jit(solution)/shard_map/ppermute | solution.py:488
  141.7 93.5 %all-to-all-start.2 = ((bf16[128,16,704]{2,1,0:T(8,128)(2,1)}), bf16[128,16,704]{2,1,0:T(8,128)(2,1)S(1)}, u32[]{:S(2)}, u32[]{:S(2)}) async-start(bf16[128,16,704]{2,1,0:T(8,128)(2,1)} %bitcast.25), calls=%async_computation.2 | async-start | bytes 6291456 | tf_op jit(solution)/shard_map/all_to_all | solution.py:482
  164.7 2.2 copy-start
  171.9 28.8 %collective-permute-start.1 = (bf16[2,4,24,1408]{3,2,1,0:T(8,128)(2,1)S(1)}, bf16[2,4,24,1408]{3,2,1,0:T(8,128)(2,1)S(1)}, u32[]{:S(2)}, u32[]{:S(2)}) collective-permute-start(bf16[2,4,24,1408]{3,2,1,0:T(8,128)(2,1)S(1)} %get-tuple-element.48), channel_id=1, source_target_pairs={{0,16},{2,18},{4,20},{6,22},{8,24},{10,26},{12,28},{14,30},{16,32}... | collective-permute-start | bytes 1622024 | tf_op jit(solution)/shard_map/ppermute | solution.py:423
  173.5 38.9 %collective-permute-start.2 = (bf16[2,4,24,1408]{3,2,1,0:T(8,128)(2,1)S(1)}, bf16[2,4,24,1408]{3,2,1,0:T(8,128)(2,1)S(1)}, u32[]{:S(2)}, u32[]{:S(2)}) collective-permute-start(bf16[2,4,24,1408]{3,2,1,0:T(8,128)(2,1)S(1)} %get-tuple-element.49), channel_id=1, source_target_pairs={{0,32},{2,34},{4,36},{6,38},{8,40},{10,42},{12,44},{14,46},{16,48}... | collective-permute-start | bytes 1622024 | tf_op jit(solution)/shard_map/ppermute | solution.py:423
  176.2 36.2 %collective-permute-start.3 = (bf16[2,4,24,1408]{3,2,1,0:T(8,128)(2,1)S(1)}, bf16[2,4,24,1408]{3,2,1,0:T(8,128)(2,1)S(1)}, u32[]{:S(2)}, u32[]{:S(2)}) collective-permute-start(bf16[2,4,24,1408]{3,2,1,0:T(8,128)(2,1)S(1)} %get-tuple-element.50), channel_id=1, source_target_pairs={{0,48},{2,50},{4,52},{6,54},{8,56},{10,58},{12,60},{14,62},{16,0},... | collective-permute-start | bytes 1622024 | tf_op jit(solution)/shard_map/ppermute | solution.py:423
  177.7 34.7 %collective-permute-start.4 = (bf16[2,4,24,1408]{3,2,1,0:T(8,128)(2,1)S(1)}, bf16[2,4,24,1408]{3,2,1,0:T(8,128)(2,1)S(1)}, u32[]{:S(2)}, u32[]{:S(2)}) collective-permute-start(bf16[2,4,24,1408]{3,2,1,0:T(8,128)(2,1)S(1)} %get-tuple-element.52), channel_id=1, source_target_pairs={{0,4},{2,6},{4,8},{6,10},{8,12},{10,14},{12,0},{14,2},{16,20},{18,... | collective-permute-start | bytes 1622024 | tf_op jit(solution)/shard_map/ppermute | solution.py:424
  179.2 34.4 %collective-permute-start.5 = (bf16[2,4,24,1408]{3,2,1,0:T(8,128)(2,1)S(1)}, bf16[2,4,24,1408]{3,2,1,0:T(8,128)(2,1)S(1)}, u32[]{:S(2)}, u32[]{:S(2)}) collective-permute-start(bf16[2,4,24,1408]{3,2,1,0:T(8,128)(2,1)S(1)} %get-tuple-element.53), channel_id=1, source_target_pairs={{0,8},{2,10},{4,12},{6,14},{8,0},{10,2},{12,4},{14,6},{16,24},{18,... | collective-permute-start | bytes 1622024 | tf_op jit(solution)/shard_map/ppermute | solution.py:424
  200.7 14.2 %collective-permute-start.6 = (bf16[2,4,24,1408]{3,2,1,0:T(8,128)(2,1)S(1)}, bf16[2,4,24,1408]{3,2,1,0:T(8,128)(2,1)S(1)}, u32[]{:S(2)}, u32[]{:S(2)}) collective-permute-start(bf16[2,4,24,1408]{3,2,1,0:T(8,128)(2,1)S(1)} %get-tuple-element.54), channel_id=1, source_target_pairs={{0,12},{2,14},{4,0},{6,2},{8,4},{10,6},{12,8},{14,10},{16,28},{18,... | collective-permute-start | bytes 1622024 | tf_op jit(solution)/shard_map/ppermute | solution.py:424
  217.2 8.2 %collective-permute-start.7 = (bf16[2,24,1408]{2,1,0:T(8,128)(2,1)S(1)}, bf16[2,24,1408]{2,1,0:T(8,128)(2,1)S(1)}, u32[]{:S(2)}, u32[]{:S(2)}) collective-permute-start(bf16[2,24,1408]{2,1,0:T(8,128)(2,1)S(1)} %get-tuple-element.56), channel_id=1, source_target_pairs={{0,4},{2,6},{4,8},{6,10},{8,12},{10,14},{12,0},{14,2},{16,20},{18,... | collective-permute-start | bytes 405512 | tf_op jit(solution)/shard_map/ppermute | solution.py:434
  218.4 9.1 %collective-permute-start.8 = (bf16[2,24,1408]{2,1,0:T(8,128)(2,1)S(1)}, bf16[2,24,1408]{2,1,0:T(8,128)(2,1)S(1)}, u32[]{:S(2)}, u32[]{:S(2)}) collective-permute-start(bf16[2,24,1408]{2,1,0:T(8,128)(2,1)S(1)} %get-tuple-element.57), channel_id=1, source_target_pairs={{0,8},{2,10},{4,12},{6,14},{8,0},{10,2},{12,4},{14,6},{16,24},{18,... | collective-permute-start | bytes 405512 | tf_op jit(solution)/shard_map/ppermute | solution.py:434
  222.5 5.1 %collective-permute-start.9 = (bf16[2,24,1408]{2,1,0:T(8,128)(2,1)S(1)}, bf16[2,24,1408]{2,1,0:T(8,128)(2,1)S(1)}, u32[]{:S(2)}, u32[]{:S(2)}) collective-permute-start(bf16[2,24,1408]{2,1,0:T(8,128)(2,1)S(1)} %get-tuple-element.58), channel_id=1, source_target_pairs={{0,12},{2,14},{4,0},{6,2},{8,4},{10,6},{12,8},{14,10},{16,28},{18,... | collective-permute-start | bytes 405512 | tf_op jit(solution)/shard_map/ppermute | solution.py:434
  222.6 7.7 %collective-permute-start.10 = (bf16[2,24,1408]{2,1,0:T(8,128)(2,1)S(1)}, bf16[2,24,1408]{2,1,0:T(8,128)(2,1)S(1)}, u32[]{:S(2)}, u32[]{:S(2)}) collective-permute-start(bf16[2,24,1408]{2,1,0:T(8,128)(2,1)S(1)} %get-tuple-element.60), channel_id=1, source_target_pairs={{0,16},{2,18},{4,20},{6,22},{8,24},{10,26},{12,28},{14,30},{16,32}... | collective-permute-start | bytes 405512 | tf_op jit(solution)/shard_map/ppermute | solution.py:435
  222.6 7.7 %collective-permute-start.11 = (bf16[2,24,1408]{2,1,0:T(8,128)(2,1)S(1)}, bf16[2,24,1408]{2,1,0:T(8,128)(2,1)S(1)}, u32[]{:S(2)}, u32[]{:S(2)}) collective-permute-start(bf16[2,24,1408]{2,1,0:T(8,128)(2,1)S(1)} %get-tuple-element.61), channel_id=1, source_target_pairs={{0,32},{2,34},{4,36},{6,38},{8,40},{10,42},{12,44},{14,46},{16,48}... | collective-permute-start | bytes 405512 | tf_op jit(solution)/shard_map/ppermute | solution.py:435
  225.4 5.7 %collective-permute-start.12 = (bf16[2,24,1408]{2,1,0:T(8,128)(2,1)S(1)}, bf16[2,24,1408]{2,1,0:T(8,128)(2,1)S(1)}, u32[]{:S(2)}, u32[]{:S(2)}) collective-permute-start(bf16[2,24,1408]{2,1,0:T(8,128)(2,1)S(1)} %get-tuple-element.62), channel_id=1, source_target_pairs={{0,48},{2,50},{4,52},{6,54},{8,56},{10,58},{12,60},{14,62},{16,0},... | collective-permute-start | bytes 405512 | tf_op jit(solution)/shard_map/ppermute | solution.py:435
  232.5 5.9 %collective-permute-start.13 = (bf16[2,24,1408]{2,1,0:T(8,128)(2,1)}, bf16[2,24,1408]{2,1,0:T(8,128)(2,1)S(1)}, u32[]{:S(2)}, u32[]{:S(2)}) collective-permute-start(bf16[2,24,1408]{2,1,0:T(8,128)(2,1)} %get-tuple-element.64), channel_id=1, source_target_pairs={{0,64},{2,66},{4,68},{6,70},{8,72},{10,74},{12,76},{14,78},{16,80}... | collective-permute-start | bytes 405512 | tf_op jit(solution)/shard_map/ppermute | solution.py:437

commit v3 on v0

v3 whole, which is shorter than its diff:
```python
import functools

import jax
import jax.numpy as jnp
from jax import lax
from jax.experimental import pallas as pl
from jax.experimental.pallas import tpu as pltpu
from jax.sharding import PartitionSpec as P

HEAD_DIM = 88
P_SIZE = 256
MIB = 1024 * 1024
BF = jnp.bfloat16
F32 = jnp.float32
NN = (((1,), (0,)), ((), ()))
NT = (((1,), (1,)), ((), ()))
TN = (((0,), (0,)), ((), ()))


def mm(a, b, dims=NN):
    return lax.dot_general(a, b, dims, preferred_element_type=F32)


def onehot(rows, cols, match):
    r = lax.broadcasted_iota(jnp.int32, (rows, cols), 0)
    c = lax.broadcasted_iota(jnp.int32, (rows, cols), 1)
    return jnp.where(match(r, c), 1.0, 0.0).astype(BF)


def hint(flops, size):
    return pl.CostEstimate(flops=flops, bytes_accessed=size, transcendentals=0)


def params(mib):
    return pltpu.CompilerParams(vmem_limit_bytes=mib * MIB)


def pack_kernel(x_ref, c_ref, o_ref, perm_ref):
    width = x_ref.shape[2]

    @pl.when(pl.program_id(0) == 0)
    def _():
        perm_ref[...] = onehot(
            512,
            512,
            lambda r, c: ((r >> 4) == ((c >> 1) & 31))
            & (((r >> 3) & 1) == (c >> 8))
            & (((r >> 2) & 1) == (c & 1))
            & ((r & 3) == ((c >> 6) & 3)),
        )

    rows = jnp.concatenate([x_ref[...].reshape(256, width), c_ref[...].reshape(256, width)], axis=0)
    o_ref[...] = mm(perm_ref[...], rows).astype(BF)


def pack(x, c, part):
    tokens, width = x.shape
    spec = pl.BlockSpec((4, 64, width), lambda b: (0, 2 * part + b, 0))
    return pl.pallas_call(
        pack_kernel,
        grid=(2,),
        in_specs=[spec, spec],
        out_specs=pl.BlockSpec((512, width), lambda b: (b, 0)),
        out_shape=jax.ShapeDtypeStruct((tokens, width), BF),
        scratch_shapes=[pltpu.VMEM((512, 512), BF)],
        compiler_params=params(60),
        cost_estimate=hint(10**6, 10**6),
        name="pack_rows",
    )(x.reshape(4, P_SIZE, width), c.reshape(4, P_SIZE, width))


def turn_kernel(w_ref, halves_ref):
    half = halves_ref.shape[2]
    halves_ref[0] = w_ref[:, :half]
    halves_ref[1] = w_ref[:, half:]


def turn_weights(w):
    cols, width = w.shape
    return pl.pallas_call(
        turn_kernel,
        grid=(3,),
        in_specs=[pl.BlockSpec((cols // 3, width), lambda j: (j, 0))],
        out_specs=pl.BlockSpec((2, cols // 3, width // 2), lambda j: (0, j, 0)),
        out_shape=jax.ShapeDtypeStruct((2, cols, width // 2), BF),
        compiler_params=params(60),
        cost_estimate=hint(10**6, 10**6),
        name="turn_weights",
    )(w)


def spread(from_ref, to_ref, rows, offset):
    for core in range(2):
        for place in range(32):
            device = 2 * place + core
            to_ref[core, place * 24 + offset : place * 24 + offset + rows, :] = from_ref[device * rows : (device + 1) * rows, :]


def attend_kernel(
    x_any,
    w_any,
    wo_any,
    xt_ref,
    low_ref,
    high_ref,
    dqkv_ref,
    cot_ref,
    sorted_ref,
    qkv_ref,
    grad_ref,
    turned_ref,
    wide_ref,
    attn_ref,
    upper_ref,
    lower_ref,
    patch_ref,
    x_ref,
    w_ref,
    wo_ref,
    sems,
):
    heads = grad_ref.shape[0]
    local = heads * HEAD_DIM
    scale = HEAD_DIM ** -0.5
    p = pl.program_id(0)
    copies = [
        pltpu.make_async_copy(source, target, sems.at[n])
        for n, (source, target) in enumerate(((x_any, x_ref), (w_any, w_ref), (wo_any, wo_ref)))
    ]

    @pl.when(p == 0)
    def _():
        for copy in copies:
            copy.start()
        copies[0].wait()
        perm = onehot(
            256,
            256,
            lambda r, c: ((r >> 6) == ((c >> 2) & 3)) & (((r >> 2) & 15) == (c >> 4)) & ((r & 3) == (c & 3)),
        )
        for b in range(4):
            part = mm(perm, x_ref[b * 256 : (b + 1) * 256, :]).astype(BF)
            for q in range(4):
                sorted_ref[q, b * 64 : (b + 1) * 64, :] = part[q * 64 : (q + 1) * 64, :]
        wide_ref[...] = jnp.zeros_like(wide_ref)
        upper_ref[...] = jnp.zeros_like(upper_ref)
        lower_ref[...] = jnp.zeros_like(lower_ref)
        copies[1].wait()
        copies[2].wait()

    xt = sorted_ref[p].T
    for j in range(3):
        part = mm(w_ref[j * local : (j + 1) * local, :], xt)
        qkv_ref[j * heads : (j + 1) * heads] = part.reshape(heads, HEAD_DIM, 256).astype(BF)
    cot = sorted_ref[2 + p]
    cot_ref[0] = cot
    grad_ref[...] = mm(wo_ref[...], cot.T).reshape(heads, HEAD_DIM, 256).astype(BF)
    turned_ref[...] = xt.astype(F32)
    spread(turned_ref, wide_ref, 22, 0)
    xt_ref[...] = wide_ref[...].astype(BF)
    for h in range(heads):
        query = qkv_ref[h]
        key = qkv_ref[heads + h]
        value = qkv_ref[2 * heads + h]
        gout = grad_ref[h]
        scores = mm(key.T, query) * scale
        expo = jnp.exp(scores - jnp.max(scores, axis=0, keepdims=True))
        prob = expo / jnp.sum(expo, axis=0, keepdims=True)
        weights = prob.astype(BF)
        attn_ref[h * HEAD_DIM : (h + 1) * HEAD_DIM, :] = mm(value, weights)
        dvalue = mm(gout, weights, NT)
        dweights = mm(value.T, gout)
        mean = jnp.sum(prob * dweights, axis=0, keepdims=True)
        dscores = (prob * (dweights - mean) * scale).astype(BF)
        dquery = mm(key, dscores)
        dkey = mm(query, dscores, NT)
        for j, term in enumerate((dquery, dkey, dvalue)):
            at = j * local + h * HEAD_DIM
            patch_ref[at : at + HEAD_DIM, :] = term
    dqkv_ref[0, :, : 3 * local] = patch_ref[...].astype(BF).T
    dqkv_ref[0, :, 3 * local :] = jnp.zeros((256, dqkv_ref.shape[2] - 3 * local), BF)
    spread(attn_ref, upper_ref, 11, 0)
    spread(attn_ref, lower_ref, 11, 11)
    low_ref[...] = upper_ref[...].astype(BF)
    high_ref[...] = lower_ref[...].astype(BF)


def attend(x, w, wo):
    tokens, width = x.shape
    local = wo.shape[0]
    heads = local // HEAD_DIM
    cols = -(-3 * local // 128) * 128
    spread_spec = pl.BlockSpec((2, 768, 256), lambda p: (0, 0, p))
    spread_shape = jax.ShapeDtypeStruct((2, 768, 512), BF)
    return pl.pallas_call(
        attend_kernel,
        grid=(2,),
        in_specs=[pl.BlockSpec(memory_space=pl.ANY)] * 3,
        out_specs=[
            spread_spec,
            spread_spec,
            spread_spec,
            pl.BlockSpec((1, 256, cols), lambda p: (p, 0, 0)),
            pl.BlockSpec((1, 256, width), lambda p: (p, 0, 0)),
        ],
        out_shape=[
            spread_shape,
            spread_shape,
            spread_shape,
            jax.ShapeDtypeStruct((2, 256, cols), BF),
            jax.ShapeDtypeStruct((2, 256, width), BF),
        ],
        scratch_shapes=[
            pltpu.VMEM((4, 256, width), BF),
            pltpu.VMEM((3 * heads, HEAD_DIM, 256), BF),
            pltpu.VMEM((heads, HEAD_DIM, 256), BF),
            pltpu.VMEM((width, 256), F32),
            pltpu.VMEM((2, 768, 256), F32),
            pltpu.VMEM((local, 256), F32),
            pltpu.VMEM((2, 768, 256), F32),
            pltpu.VMEM((2, 768, 256), F32),
            pltpu.VMEM((3 * local, 256), F32),
            pltpu.VMEM(x.shape, BF),
            pltpu.VMEM(w.shape, BF),
            pltpu.VMEM(wo.shape, BF),
            pltpu.SemaphoreType.DMA((3,)),
        ],
        compiler_params=params(60),
        cost_estimate=hint(10**6, 10**6),
        name="attend",
    )(x, w, wo)


def input_kernel(first_any, second_any, w_any, send_any, dqkv_ref, w_ref, rows_ref, part_ref, sems):
    cols, half = w_ref.shape[1:]
    copies = [
        pltpu.make_async_copy(source, target, sems.at[n])
        for n, (source, target) in enumerate(
            (
                (first_any, dqkv_ref.at[0:2]),
                (second_any, dqkv_ref.at[2:4]),
                (w_any.at[0], w_ref.at[0]),
                (w_any.at[1], w_ref.at[1]),
            )
        )
    ]
    for copy in copies:
        copy.start()
    perm = onehot(
        256,
        256,
        lambda r, c: ((c >> 6) == ((r >> 2) & 3)) & (((c >> 2) & 15) == (r >> 4)) & ((r & 3) == (c & 3)),
    )
    copies[0].wait()
    copies[1].wait()
    for b in range(4):
        rows = dqkv_ref[:, b * 64 : (b + 1) * 64, :cols].reshape(256, cols)
        rows_ref[b * 256 : (b + 1) * 256, :] = mm(perm, rows).astype(BF)
    outs = [pltpu.make_async_copy(part_ref.at[t], send_any.at[:, t], sems.at[4 + t]) for t in range(2)]
    for t in range(2):
        copies[2 + t].wait()
        for b in range(2):
            part = mm(rows_ref[b * 512 : (b + 1) * 512, :], w_ref[t])
            part_ref[t, b * 32 : (b + 1) * 32] = part.astype(BF).reshape(32, 16, half)
        outs[t].start()
    for out in outs:
        out.wait()


def input_grads(first, second, w):
    cols, half = w.shape[1:]
    hbm = pl.BlockSpec(memory_space=pl.ANY)
    return pl.pallas_call(
        input_kernel,
        in_specs=[hbm, hbm, hbm],
        out_specs=hbm,
        out_shape=jax.ShapeDtypeStruct((64, 2, 16, half), BF),
        scratch_shapes=[
            pltpu.VMEM((4, *first.shape[1:]), BF),
            pltpu.VMEM(w.shape, BF),
            pltpu.VMEM((1024, cols), BF),
            pltpu.VMEM((2, 64, 16, half), BF),
            pltpu.SemaphoreType.DMA((6,)),
        ],
        compiler_params=params(60),
        cost_estimate=hint(10**6, 10**6),
        name="input_grads",
    )(first, second, w)


def weights_kernel(core_ref, xt_ref, low_ref, high_ref, dqkv_ref, c_ref, *refs):
    o_ref = refs[-1]
    places = o_ref.shape[0]
    half = c_ref.shape[1] // 2
    cols = 3 * half

    def put(value, at):
        value = value.reshape(places, 24, value.shape[1])
        if len(refs) == 2:
            value += refs[0][:, :, at].astype(F32)
        o_ref[:, :, at] = value.astype(BF)

    put(mm(xt_ref[0], dqkv_ref[:, :cols]), slice(0, cols))
    put(mm(low_ref[0], c_ref[:, :half]) + mm(high_ref[0], c_ref[:, half:]), slice(cols, cols + half))


def weight_grads(core, terms, before=None, flops=10**6):
    xt, low, high, dqkv, cot = terms
    tokens = xt.shape[2]
    dqkv, cot = dqkv.reshape(tokens, -1), cot.reshape(tokens, -1)
    width = cot.shape[1]
    once = pl.Buffered(buffer_count=1)
    rows_spec = pl.BlockSpec((1, 384, tokens), lambda s, core: (core[0], s, 0))
    out_spec = pl.BlockSpec((16, 24, 2 * width), lambda s, core: (s, 0, 0))
    given = [] if before is None else [before]
    return pl.pallas_call(
        weights_kernel,
        grid_spec=pltpu.PrefetchScalarGridSpec(
            num_scalar_prefetch=1,
            grid=(2,),
            in_specs=[
                rows_spec,
                rows_spec,
                rows_spec,
                pl.BlockSpec(dqkv.shape, lambda s, core: (0, 0), pipeline_mode=once),
                pl.BlockSpec(cot.shape, lambda s, core: (0, 0), pipeline_mode=once),
            ]
            + [out_spec] * len(given),
            out_specs=out_spec,
        ),
        out_shape=jax.ShapeDtypeStruct((32, 24, 2 * width), BF),
        compiler_params=params(60),
        cost_estimate=hint(flops, 10**6),
        name="weight_grads",
    )(core, xt, low, high, dqkv, cot, *given)


def core_kernel(at_ref, mine_low, other_low, mine_high, other_high, *outs):
    k = pl.program_id(0)
    for group, terms in enumerate(((mine_low, other_low), (mine_high, other_high))):
        total = (terms[0][...].astype(F32) + terms[1][...].astype(F32)).astype(BF).reshape(outs[0].shape)
        own, after, before, left, right = outs[5 * group : 5 * group + 5]

        @pl.when(k == 0)
        def _():
            own[...] = total

        @pl.when(k == 1)
        def _():
            after[...] = total

        @pl.when(k == 3)
        def _():
            before[...] = total

        @pl.when(k == 2)
        def _():
            left[...] = total[0]
            right[...] = total[1]


def core_sum(at, mine, arrived):
    width = mine.shape[4] // 2
    shape = (2, 4, 24, width)
    low = pl.BlockSpec((2, 1, 4, 24, width), lambda k, at: (0, (at[0] + k) % 4, 0, 0, 0))
    high = pl.BlockSpec((2, 4, 1, 24, width), lambda k, at: (0, 0, (at[1] + k) % 4, 0, 1))
    shapes = ([shape] * 3 + [shape[1:]] * 2) * 2
    return pl.pallas_call(
        core_kernel,
        grid_spec=pltpu.PrefetchScalarGridSpec(
            num_scalar_prefetch=1,
            grid=(4,),
            in_specs=[low, low, high, high],
            out_specs=[pl.BlockSpec(shape, lambda k, at, n=len(shape): (0,) * n) for shape in shapes],
        ),
        out_shape=[jax.ShapeDtypeStruct(shape, BF) for shape in shapes],
        compiler_params=params(40),
        cost_estimate=hint(10**6, 10**6),
        name="core_sum",
    )(at, mine, arrived, mine, arrived)


def pass_kernel(*refs):
    ins, outs = refs[:8], refs[8:]
    for group in range(2):
        after, before, left, right = ins[4 * group : 4 * group + 4]
        outs[2 * group][0] = (after[0].astype(F32) + left[...].astype(F32)).astype(BF)
        outs[2 * group][1] = after[1]
        outs[2 * group + 1][0] = before[0]
        outs[2 * group + 1][1] = (before[1].astype(F32) + right[...].astype(F32)).astype(BF)


def pass_on(*terms):
    return pl.pallas_call(
        pass_kernel,
        out_shape=[jax.ShapeDtypeStruct(terms[0].shape, BF)] * 4,
        compiler_params=params(24),
        cost_estimate=hint(10**6, 10**6),
        name="pass_on",
    )(*terms)


def ring_kernel(at_ref, *refs):
    k = pl.program_id(0)
    outs = refs[6:]
    for group in range(2):
        total = refs[3 * group][...].astype(F32)
        for term in refs[3 * group + 1 : 3 * group + 3]:
            total += term[...].astype(F32)
        for q in range(4):

            @pl.when(k == q)
            def _():
                outs[4 * group + q][...] = total.astype(BF).reshape(outs[q].shape)


def ring_sum(at, lows, highs):
    width = lows[0].shape[3]
    shape = (2, 24, width)
    low = pl.BlockSpec((2, 1, 24, width), lambda k, at: (0, (at[1] + k) % 4, 0, 0))
    high = pl.BlockSpec((2, 1, 24, width), lambda k, at: (0, (at[0] + k) % 4, 0, 0))
    return pl.pallas_call(
        ring_kernel,
        grid_spec=pltpu.PrefetchScalarGridSpec(
            num_scalar_prefetch=1,
            grid=(4,),
            in_specs=[low] * 3 + [high] * 3,
            out_specs=[pl.BlockSpec(shape, lambda k, at: (0, 0, 0))] * 8,
        ),
        out_shape=[jax.ShapeDtypeStruct(shape, BF)] * 8,
        compiler_params=params(40),
        cost_estimate=hint(10**6, 10**6),
        name="ring_sum",
    )(at, *lows, *highs)


def pair_kernel(at_ref, *refs):
    mine_ref, other_ref = refs[8:]
    for group in range(2):
        total = refs[4 * group][...].astype(F32)
        for term in refs[4 * group + 1 : 4 * group + 4]:
            total += term[...].astype(F32)
        z = at_ref[2]
        mine_ref[group] = jnp.where(z == 0, total[0], total[1])
        other_ref[group] = jnp.where(z == 0, total[1], total[0]).astype(BF)


def pair_sum(at, terms):
    shape = terms[0].shape
    return pl.pallas_call(
        pair_kernel,
        in_specs=[pl.BlockSpec(memory_space=pltpu.SMEM)] + [pl.BlockSpec(memory_space=pltpu.VMEM)] * 8,
        out_shape=[jax.ShapeDtypeStruct(shape, F32), jax.ShapeDtypeStruct(shape, BF)],
        compiler_params=params(16),
        name="pair_sum",
    )(at, *terms)


def final_kernel(mine_ref, other_ref, qkv_ref, out_ref):
    half = out_ref.shape[1] // 2
    low = mine_ref[0] + other_ref[0].astype(F32)
    high = mine_ref[1] + other_ref[1].astype(F32)
    qkv_ref[0] = low[:22, :half]
    qkv_ref[1] = low[:22, half:]
    qkv_ref[2] = high[:22, :half]
    out_ref[:, :half] = high[:11, half:]
    out_ref[:, half:] = high[11:22, half:]


def final_sum(mine, other):
    width = mine.shape[2]
    return pl.pallas_call(
        final_kernel,
        out_shape=[jax.ShapeDtypeStruct((3, 22, width // 2), F32), jax.ShapeDtypeStruct((11, width), F32)],
        compiler_params=params(16),
        name="final_sum",
    )(mine, other)


def sum_over_chips(mine, arrived, at, beside):
    width = mine.shape[1] // 2
    mine, arrived = (a.reshape(2, 4, 4, 24, 2 * width) for a in (mine, arrived))

    def to(step_x, step_y, flip=0):
        pairs = []
        for i in range(64):
            z, x, y, core = i // 32, i // 8 % 4, i // 2 % 4, i % 2
            pairs.append((i, (((z ^ flip) * 4 + (x + step_x) % 4) * 4 + (y + step_y) % 4) * 2 + core))
        return pairs

    first = core_sum(at, mine, arrived)
    steps = ((1, 0), (-1, 0), (0, 1), (0, -1))
    halves = [lax.ppermute(first[n], "seq", to(*step)) for n, step in zip((3, 4, 8, 9), steps)]
    passed = pass_on(first[1], first[2], *halves[:2], first[6], first[7], *halves[2:])
    passed = [lax.ppermute(value, "seq", to(*step)) for value, step in zip(passed, steps)]
    second = ring_sum(at, [first[0], *passed[:2]], [first[5], *passed[2:]])
    lows = [second[0]] + [lax.ppermute(second[k], "seq", to(0, k)) for k in (1, 2, 3)]
    highs = [second[4]] + [lax.ppermute(second[4 + k], "seq", to(k, 0)) for k in (1, 2, 3)]
    kept, given = pair_sum(at, lows + highs)
    return (*final_sum(kept, lax.ppermute(given, "seq", to(0, 0, 1))), beside)


def unpack_kernel(x_ref, o_ref):
    half = x_ref.shape[2]
    pick = onehot(
        1024,
        512,
        lambda r, c: ((r & 3) == (c >> 7)) & ((r >> 4) == ((c >> 1) & 63)) & (((r >> 2) & 1) == (c & 1)),
    )
    rows = x_ref[...].astype(F32)
    for n in range(2):
        part = rows[:, n * 8 : (n + 1) * 8].reshape(1024, half).astype(BF)
        part = mm(part.T, pick).astype(BF)
        for f in range(4):
            o_ref[:, f * 256 + n * 128 : f * 256 + (n + 1) * 128] = part[:, f * 128 : (f + 1) * 128]


def unpack(x):
    half = x.shape[2]
    return pl.pallas_call(
        unpack_kernel,
        out_shape=jax.ShapeDtypeStruct((half, 1024), BF),
        compiler_params=params(32),
        cost_estimate=hint(10**6, 10**6),
        name="unpack_rows",
    )(x)


def shards(hidden, out_cotangent, qkv_weight, out_weight):
    tokens, width = hidden.shape
    local = qkv_weight.shape[2]
    n_seq = lax.axis_size("seq")
    w_rows = qkv_weight.transpose(1, 2, 0).reshape(3 * local, width)
    place = lax.axis_index("seq").astype(jnp.int32)
    core = (place % 2).reshape(1)
    at = jnp.stack([place // 8 % 4, place // 2 % 4, place // 32])

    def to_patches(rows):
        return lax.all_to_all(rows.reshape(n_seq, 16, width), "seq", split_axis=0, concat_axis=0, tiled=True).reshape(tokens, width)

    def to_frames(rows):
        rows = rows.reshape(2 * n_seq, 16, width // 2)
        return lax.all_to_all(rows, ("seq", "tp"), split_axis=0, concat_axis=0, tiled=True)

    w_halves = turn_weights(w_rows)
    arrived = to_patches(pack(hidden, out_cotangent, 0))
    send = pack(hidden, out_cotangent, 1)
    arrived, send, w_halves = lax.optimization_barrier((arrived, send, w_halves))
    second = to_patches(send)
    terms = attend(arrived, w_rows, out_weight)
    other = weight_grads(1 - core, terms)
    mine = weight_grads(core, terms)
    dqkv = terms[3]
    second, other, mine, dqkv = lax.optimization_barrier((second, other, mine, dqkv))
    terms = attend(second, w_rows, out_weight)
    sending = input_grads(dqkv, terms[3], w_halves)
    terms, sending = lax.optimization_barrier((terms, sending))
    returned = to_frames(sending)
    other = weight_grads(1 - core, terms, other)
    from_peer = lax.ppermute(other, "seq", [(i, i ^ 1) for i in range(n_seq)])
    mine = weight_grads(core, terms, mine, 10**11)
    shape = (32 * 24, 2 * width)
    qkv_grad, out_grad, returned = sum_over_chips(mine.reshape(shape), from_peer.reshape(shape), at, returned)
    return (unpack(returned).T, qkv_grad.transpose(1, 0, 2), out_grad)


def solution(mesh):
    return jax.shard_map(
        shards,
        mesh=mesh,
        in_specs=(P("seq", None), P("seq", None), P(None, None, "tp"), P("tp", None)),
        out_specs=(P("seq", "tp"), P("seq", None, "tp"), P(("tp", "seq"), None)),
        check_vma=False,
    )
```

time: 1030 us -> 234 us (0.23)
  blocking collectives: 379 us -> 0 us
  waiting for transfers between devices: 330 us -> 61.4 us
  local copies, waits for them, and re-layouts: 139 us -> 5.43 us
  Pallas kernels: 0 us -> 115 us
  matrix products: 95.2 us -> 0 us
  between operations: 17.7 us -> 1.23 us
  other arithmetic: 14.3 us -> 0.08 us
    unnamed x23 -> x0, waiting for transfers between devices: 330 us -> none
    all_to_all x2 -> x0, blocking collectives: 209 us -> none  [the longest x1 106 us: shards(): lax.all_to_all(stacked, 'seq', split_axis=1, concat_axis=0, tiled=True)]
    unnamed x1 -> x0, blocking collectives: 170 us -> none
    pallas_call x0 -> x16, Pallas kernels: none -> 115 us  [the longest x2 41.8 us: attend(): pl.pallas_call(attend_kernel, grid=(2,), in_specs=[pl.BlockSpec(memory_sp...]
    dot_general x11 -> x0, matrix products: 95.2 us -> none  [the longest x1 15.5 us: shards(): jnp.einsum('tc,tf->cf', columns, dqkv, preferred_element_type=jnp.float32)]
    unnamed x42 -> x6, local copies, waits for them, and re-layouts: 58.5 us -> 5.43 us
    unnamed x21 -> x0, starting transfers between devices: 50.5 us -> none
    reshape x3 -> x0, local copies, waits for them, and re-layouts: 41.5 us -> none  [the longest x2 25.8 us: shards(): stacked = stacked.reshape(frames_here, P_SIZE, 4, heads_here, HEAD_DIM)]
  transfers between devices with their start and end apart: 22 -> 19, of which waited for: 8 -> 13; matrix products, arithmetic and copies ran while one was open for 22% -> 0% of each run, Pallas kernels for 0% -> 33%
where the time goes in v3:
time: 234 us; the launch traced here: 230 us
  Pallas kernels  115 us (49%)
  waiting for transfers between devices  61.4 us (26%)
  starting transfers between devices  46.7 us (20%)
  local copies, waits for them, and re-layouts  5.43 us (2%)
    pallas_call x2, Pallas kernels, attend(): pl.pallas_call(attend_kernel, grid=(2,), in_specs=[pl.BlockSpec(memory_sp...  41.8 us
    pallas_call x4, Pallas kernels, weight_grads(): pl.pallas_call(weights_kernel, grid_spec=pltpu.PrefetchScalarGridSpec(num...  31.3 us
    all_to_all x2, waiting for transfers between devices, to_patches(): lax.all_to_all(rows.reshape(n_seq, 16, width), 'seq', split_axis=0, conca...  26.4 us
    all_to_all x2, starting transfers between devices, to_patches(): lax.all_to_all(rows.reshape(n_seq, 16, width), 'seq', split_axis=0, conca...  17.8 us
    ppermute x4, waiting for transfers between devices, sum_over_chips(): lax.ppermute(value, 'seq', to(*step))  13.2 us
    ppermute x4, waiting for transfers between devices, sum_over_chips(): lax.ppermute(first[n], 'seq', to(*step))  12.7 us
    pallas_call x1, Pallas kernels, input_grads(): pl.pallas_call(input_kernel, in_specs=[hbm, hbm, hbm], out_specs=hbm, out...  12.6 us
    pallas_call x2, Pallas kernels, pack(): pl.pallas_call(pack_kernel, grid=(2,), in_specs=[spec, spec], out_specs=p...  9.7 us
  transfers between devices with their start and end apart: 19, of which 13 were waited for; matrix products, arithmetic and copies ran while one was open for 0% of the time, Pallas kernels for 33%

profile of v3, /device:TPU:32, one launch (start us, length us, event | category | flops | bytes accessed | tf_op | source)
XLA Modules:
  0.0 229.5 jit_solution(13405531996821634043)
XLA Ops:
  0.6 4.9 %pack_rows.2 = bf16[1024,1408]{1,0:T(8,128)(2,1)} custom-call(bf16[4,256,1408]{2,1,0:T(8,128)(2,1)} %bitcast.30, bf16[4,256,1408]{2,1,0:T(8,128)(2,1)} %bitcast.32), custom_call_target="tpu_custom_call" | custom-call | flops 1000000 | bytes 1000000 | tf_op jit(solution)/shard_map/pack_rows/pallas_call | solution.py:59
  5.5 9.0 %all-to-all-start = ((bf16[64,16,1408]{2,1,0:T(8,128)(2,1)}), bf16[64,16,1408]{2,1,0:T(8,128)(2,1)S(1)}, u32[]{:S(2)}, u32[]{:S(2)}) async-start(bf16[64,16,1408]{2,1,0:T(8,128)(2,1)} %bitcast.34), calls=%async_computation | async-start | bytes 5767168 | tf_op jit(solution)/shard_map/all_to_all | solution.py:539
  14.6 4.8 %pack_rows.3 = bf16[1024,1408]{1,0:T(8,128)(2,1)} custom-call(bf16[4,256,1408]{2,1,0:T(8,128)(2,1)} %bitcast.31, bf16[4,256,1408]{2,1,0:T(8,128)(2,1)} %bitcast.33), custom_call_target="tpu_custom_call" | custom-call | flops 1000000 | bytes 1000000 | tf_op jit(solution)/shard_map/pack_rows/pallas_call | solution.py:59
  19.4 6.9 %turn_weights.1.w_any = bf16[2,2112,704]{2,1,0:T(8,128)(2,1)} custom-call(bf16[2112,1408]{1,0:T(8,128)(2,1)} %bitcast.24), custom_call_target="tpu_custom_call" | custom-call | flops 1000000 | bytes 1000000 | tf_op jit(solution)/shard_map/turn_weights/pallas_call | solution.py:80
  26.2 25.4 %all-to-all-done = bf16[64,16,1408]{2,1,0:T(8,128)(2,1)S(1)} async-done(((bf16[64,16,1408]{2,1,0:T(8,128)(2,1)}), bf16[64,16,1408]{2,1,0:T(8,128)(2,1)S(1)}, u32[]{:S(2)}, u32[]{:S(2)}) %all-to-all-start) | async-done | bytes 2883616 | tf_op jit(solution)/shard_map/all_to_all | solution.py:539
  51.6 0.0 copy-start.2
  51.7 1.6 copy-done.2
  53.3 8.7 %all-to-all-start.1 = ((bf16[64,16,1408]{2,1,0:T(8,128)(2,1)}), bf16[64,16,1408]{2,1,0:T(8,128)(2,1)S(1)}, u32[]{:S(2)}, u32[]{:S(2)}) async-start(bf16[64,16,1408]{2,1,0:T(8,128)(2,1)} %bitcast.6), calls=%async_computation.1 | async-start | bytes 5767168 | tf_op jit(solution)/shard_map/all_to_all | solution.py:539
  62.1 0.1 pad_add_fusion.at_ref
  62.2 20.8 %attend.2 = (bf16[2,768,512]{2,1,0:T(8,128)(2,1)}, bf16[2,768,512]{2,1,0:T(8,128)(2,1)}, bf16[2,768,512]{2,1,0:T(8,128)(2,1)}, bf16[2,256,2176]{2,1,0:T(8,128)(2,1)}, bf16[2,256,1408]{2,1,0:T(8,128)(2,1)}) custom-call(bf16[1024,1408]{1,0:T(8,128)(2,1)} %bitcast.36, bf16[2112,1408]{1,0:T(8,128)(2,1)} %bitcast.25, bf16[704,1408]{1,0:T(8,128)(2,1)} %wo_any.3), custom_call_target="tpu_custom_call" | custom-call | flops 1000000 | bytes 1000000 | tf_op jit(solution)/shard_map/attend/pallas_call | solution.py:195
  83.0 7.5 %weight_grads.5.refs_0_ = bf16[32,24,2816]{2,1,0:T(8,128)(2,1)} custom-call(s32[1]{0:T(128)} %bitcast.8.core_ref, bf16[2,768,512]{2,1,0:T(8,128)(2,1)} %get-tuple-element.54.xt_ref, bf16[2,768,512]{2,1,0:T(8,128)(2,1)} %get-tuple-element.55.low_ref, bf16[2,768,512]{2,1,0:T(8,128)(2,1)} %get-tuple-element.56.high_ref, bf16[512,2176]{1,0:T(8,128)(2,1)} %bitcast.27, ...), custom_call_target="tpu_custom_call" | custom-call | flops 1000000 | bytes 1000000 | tf_op jit(solution)/shard_map/weight_grads/pallas_call | solution.py:316
  90.5 7.5 %weight_grads.4.refs_0_ = bf16[32,24,2816]{2,1,0:T(8,128)(2,1)} custom-call(s32[1]{0:T(128)S(6)} %sub.14.core_ref, bf16[2,768,512]{2,1,0:T(8,128)(2,1)} %get-tuple-element.54.xt_ref, bf16[2,768,512]{2,1,0:T(8,128)(2,1)} %get-tuple-element.55.low_ref, bf16[2,768,512]{2,1,0:T(8,128)(2,1)} %get-tuple-element.56.high_ref, bf16[512,2176]{1,0:T(8,128)(2,1)} %bitcast.28, ...), custom_call_target="tpu_custom_call" | custom-call | flops 1000000 | bytes 1000000 | tf_op jit(solution)/shard_map/weight_grads/pallas_call | solution.py:316
  98.0 1.0 all-to-all-done.1
  99.1 0.0 copy-start.1
  99.1 1.6 copy-done.1
  100.6 21.0 %attend.3 = (bf16[2,768,512]{2,1,0:T(8,128)(2,1)}, bf16[2,768,512]{2,1,0:T(8,128)(2,1)}, bf16[2,768,512]{2,1,0:T(8,128)(2,1)}, bf16[2,256,2176]{2,1,0:T(8,128)(2,1)}, bf16[2,256,1408]{2,1,0:T(8,128)(2,1)}) custom-call(bf16[1024,1408]{1,0:T(8,128)(2,1)} %bitcast.35, bf16[2112,1408]{1,0:T(8,128)(2,1)} %bitcast.26, bf16[704,1408]{1,0:T(8,128)(2,1)} %wo_any.3), custom_call_target="tpu_custom_call" | custom-call | flops 1000000 | bytes 1000000 | tf_op jit(solution)/shard_map/attend/pallas_call | solution.py:195
  121.6 12.6 %input_grads.1 = bf16[64,2,16,704]{3,2,1,0:T(8,128)(2,1)} custom-call(bf16[2,256,2176]{2,1,0:T(8,128)(2,1)} %get-tuple-element.65.first_any, bf16[2,256,2176]{2,1,0:T(8,128)(2,1)} %get-tuple-element.71.second_any, bf16[2,2112,704]{2,1,0:T(8,128)(2,1)} %turn_weights.1.w_any), custom_call_target="tpu_custom_call" | custom-call | flops 1000000 | bytes 1000000 | tf_op jit(solution)/shard_map/input_grads/pallas_call | solution.py:273
  134.3 9.5 %all-to-all-start.2 = ((bf16[128,16,704]{2,1,0:T(8,128)(2,1)}), bf16[128,16,704]{2,1,0:T(8,128)(2,1)S(1)}, u32[]{:S(2)}, u32[]{:S(2)}) async-start(bf16[128,16,704]{2,1,0:T(8,128)(2,1)} %bitcast.29), calls=%async_computation.2 | async-start | bytes 6291456 | tf_op jit(solution)/shard_map/all_to_all | solution.py:543
  143.7 8.2 %weight_grads.7 = bf16[32,24,2816]{2,1,0:T(8,128)(2,1)} custom-call(s32[1]{0:T(128)S(6)} %sub.14.core_ref, bf16[2,768,512]{2,1,0:T(8,128)(2,1)} %get-tuple-element.68.xt_ref, bf16[2,768,512]{2,1,0:T(8,128)(2,1)} %get-tuple-element.69.low_ref, bf16[2,768,512]{2,1,0:T(8,128)(2,1)} %get-tuple-element.70.high_ref, bf16[512,2176]{1,0:T(8,128)(2,1)} %bitcast.37, ...), custom_call_target="tpu_custom_call" | custom-call | flops 1000000 | bytes 1000000 | tf_op jit(solution)/shard_map/weight_grads/pallas_call | solution.py:316
  151.9 0.1 collective-permute-start
  152.0 8.1 %weight_grads.6 = bf16[32,24,2816]{2,1,0:T(8,128)(2,1)} custom-call(s32[1]{0:T(128)} %bitcast.8.core_ref, bf16[2,768,512]{2,1,0:T(8,128)(2,1)} %get-tuple-element.68.xt_ref, bf16[2,768,512]{2,1,0:T(8,128)(2,1)} %get-tuple-element.69.low_ref, bf16[2,768,512]{2,1,0:T(8,128)(2,1)} %get-tuple-element.70.high_ref, bf16[512,2176]{1,0:T(8,128)(2,1)} %bitcast.38, ...), custom_call_target="tpu_custom_call" | custom-call | flops 99999997952 | bytes 1000000 | tf_op jit(solution)/shard_map/weight_grads/pallas_call | solution.py:316
  160.2 0.0 collective-permute-done
  160.2 0.0 copy-start
  160.2 2.2 copy-done
  162.4 5.0 %core_sum.1 = (bf16[2,4,24,1408]{3,2,1,0:T(8,128)(2,1)S(1)}, bf16[2,4,24,1408]{3,2,1,0:T(8,128)(2,1)S(1)}, bf16[2,4,24,1408]{3,2,1,0:T(8,128)(2,1)S(1)}, bf16[4,...) custom-call(s32[3]{0:T(128)S(1)} %pad_add_fusion.at_ref, ...), custom_call_target="tpu_custom_call" | custom-call | flops 1000000 | bytes 1000000 | tf_op jit(solution)/shard_map/core_sum/pallas_call | solution.py:368
  167.4 1.6 collective-permute-start.1
  169.0 1.8 collective-permute-start.2
  170.7 1.5 collective-permute-start.3
  172.3 1.7 collective-permute-start.4
  174.0 12.3 %collective-permute-done.1.refs_2_ = bf16[4,24,1408]{2,1,0:T(8,128)(2,1)S(1)} collective-permute-done((bf16[4,24,1408]{2,1,0:T(8,128)(2,1)S(1)}, bf16[4,24,1408]{2,1,0:T(8,128)(2,1)S(1)}, u32[]{:S(2)}, u32[]{:S(2)}) %collective-permute-start.1) | collective-permute-done | bytes 270368 | tf_op jit(solution)/shard_map/ppermute | solution.py:493
  186.3 0.0 collective-permute-done.2.refs_3_
  186.3 0.4 collective-permute-done.3.refs_6_
  186.7 0.0 collective-permute-done.4.refs_7_
  186.7 0.3 pass_on.1
  187.0 1.5 collective-permute-start.5
  188.5 1.8 collective-permute-start.6
  190.3 3.1 %collective-permute-start.7 = (bf16[2,4,24,1408]{3,2,1,0:T(8,128)(2,1)S(1)}, bf16[2,4,24,1408]{3,2,1,0:T(8,128)(2,1)S(1)}, u32[]{:S(2)}, u32[]{:S(2)}) collective-permute-start(bf16[2,4,24,1408]{3,2,1,0:T(8,128)(2,1)S(1)} %get-tuple-element.87), channel_id=1, source_target_pairs={{0,4},{2,6},{4,8},{6,10},{8,12},{10,14},{12,0},{14,2},{16,20},{18,... | collective-permute-start | bytes 1622024 | tf_op jit(solution)/shard_map/ppermute | solution.py:495
  193.4 0.1 collective-permute-start.8
  193.5 8.7 %collective-permute-done.5.refs_1_ = bf16[2,4,24,1408]{3,2,1,0:T(8,128)(2,1)S(1)} collective-permute-done((bf16[2,4,24,1408]{3,2,1,0:T(8,128)(2,1)S(1)}, bf16[2,4,24,1408]{3,2,1,0:T(8,128)(2,1)S(1)}, u32[]{:S(2)}, u32[]{:S(2)}) %collective-permute-start.5) | collective-permute-done | bytes 540704 | tf_op jit(solution)/shard_map/ppermute | solution.py:495
  202.3 0.2 collective-permute-done.6.refs_2_
  202.5 2.5 %collective-permute-done.7.refs_4_ = bf16[2,4,24,1408]{3,2,1,0:T(8,128)(2,1)S(1)} collective-permute-done((bf16[2,4,24,1408]{3,2,1,0:T(8,128)(2,1)S(1)}, bf16[2,4,24,1408]{3,2,1,0:T(8,128)(2,1)S(1)}, u32[]{:S(2)}, u32[]{:S(2)}) %collective-permute-start.7) | collective-permute-done | bytes 540704 | tf_op jit(solution)/shard_map/ppermute | solution.py:495
  205.0 1.7 collective-permute-done.8.refs_5_
  206.8 2.0 ring_sum.1
  208.7 0.4 collective-permute-start.9
  209.1 2.7 %collective-permute-start.10 = (bf16[2,24,1408]{2,1,0:T(8,128)(2,1)S(1)}, bf16[2,24,1408]{2,1,0:T(8,128)(2,1)S(1)}, u32[]{:S(2)}, u32[]{:S(2)}) collective-permute-start(bf16[2,24,1408]{2,1,0:T(8,128)(2,1)S(1)} %get-tuple-element.91), channel_id=1, source_target_pairs={{0,8},{2,10},{4,12},{6,14},{8,0},{10,2},{12,4},{14,6},{16,24},{18,... | collective-permute-start | bytes 405512 | tf_op jit(solution)/shard_map/ppermute | solution.py:497
  211.8 0.3 collective-permute-start.11
  212.1 0.0 collective-permute-start.12
  212.1 2.9 %collective-permute-start.13 = (bf16[2,24,1408]{2,1,0:T(8,128)(2,1)S(1)}, bf16[2,24,1408]{2,1,0:T(8,128)(2,1)S(1)}, u32[]{:S(2)}, u32[]{:S(2)}) collective-permute-start(bf16[2,24,1408]{2,1,0:T(8,128)(2,1)S(1)} %get-tuple-element.95), channel_id=1, source_target_pairs={{0,32},{2,34},{4,36},{6,38},{8,40},{10,42},{12,44},{14,46},{16,48}... | collective-permute-start | bytes 405512 | tf_op jit(solution)/shard_map/ppermute | solution.py:498
  215.0 1.7 collective-permute-done.9.refs_1_
  216.7 0.0 collective-permute-start.14
  216.7 0.0 collective-permute-done.10.refs_2_
  216.7 0.7 collective-permute-done.11.refs_3_
  217.4 2.4 %collective-permute-done.12.refs_5_ = bf16[2,24,1408]{2,1,0:T(8,128)(2,1)S(1)} collective-permute-done((bf16[2,24,1408]{2,1,0:T(8,128)(2,1)S(1)}, bf16[2,24,1408]{2,1,0:T(8,128)(2,1)S(1)}, u32[]{:S(2)}, u32[]{:S(2)}) %collective-permute-start.12) | collective-permute-done | bytes 135200 | tf_op jit(solution)/shard_map/ppermute | solution.py:498
  219.8 0.0 collective-permute-done.13.refs_6_
  219.8 1.9 collective-permute-done.14.refs_7_
  221.7 1.3 pair_sum.1
  223.0 0.0 collective-permute-start.15
  223.0 0.0 all-to-all-done.2.x_ref
  223.0 2.9 %unpack_rows.1 = bf16[704,1024]{1,0:T(8,128)(2,1)} custom-call(bf16[128,16,704]{2,1,0:T(8,128)(2,1)S(1)} %all-to-all-done.2.x_ref), custom_call_target="tpu_custom_call" | custom-call | flops 1000000 | bytes 1000000 | tf_op jit(solution)/shard_map/unpack_rows/pallas_call | solution.py:520
  226.0 2.3 %collective-permute-done.15.other_ref = bf16[2,24,1408]{2,1,0:T(8,128)(2,1)S(1)} collective-permute-done((bf16[2,24,1408]{2,1,0:T(8,128)(2,1)}, bf16[2,24,1408]{2,1,0:T(8,128)(2,1)S(1)}, u32[]{:S(2)}, u32[]{:S(2)}) %collective-permute-start.15) | collective-permute-done | bytes 135200 | tf_op jit(solution)/shard_map/ppermute | solution.py:500
  228.3 0.8 final_sum.1
Async XLA Ops:
  5.5 46.1 %all-to-all-start = ((bf16[64,16,1408]{2,1,0:T(8,128)(2,1)}), bf16[64,16,1408]{2,1,0:T(8,128)(2,1)S(1)}, u32[]{:S(2)}, u32[]{:S(2)}) async-start(bf16[64,16,1408]{2,1,0:T(8,128)(2,1)} %bitcast.34), calls=%async_computation | async-start | bytes 5767168 | tf_op jit(solution)/shard_map/all_to_all | solution.py:539
  51.6 1.6 copy-start.2
  53.3 45.8 %all-to-all-start.1 = ((bf16[64,16,1408]{2,1,0:T(8,128)(2,1)}), bf16[64,16,1408]{2,1,0:T(8,128)(2,1)S(1)}, u32[]{:S(2)}, u32[]{:S(2)}) async-start(bf16[64,16,1408]{2,1,0:T(8,128)(2,1)} %bitcast.6), calls=%async_computation.1 | async-start | bytes 5767168 | tf_op jit(solution)/shard_map/all_to_all | solution.py:539
  99.1 1.6 copy-start.1
  134.3 88.8 %all-to-all-start.2 = ((bf16[128,16,704]{2,1,0:T(8,128)(2,1)}), bf16[128,16,704]{2,1,0:T(8,128)(2,1)S(1)}, u32[]{:S(2)}, u32[]{:S(2)}) async-start(bf16[128,16,704]{2,1,0:T(8,128)(2,1)} %bitcast.29), calls=%async_computation.2 | async-start | bytes 6291456 | tf_op jit(solution)/shard_map/all_to_all | solution.py:543
  151.9 8.3 %collective-permute-start = (bf16[32,24,2816]{2,1,0:T(8,128)(2,1)}, bf16[32,24,2816]{2,1,0:T(8,128)(2,1)}, u32[]{:S(2)}, u32[]{:S(2)}) collective-permute-start(bf16[32,24,2816]{2,1,0:T(8,128)(2,1)} %weight_grads.7), channel_id=1, source_target_pairs={{0,2},{2,0},{4,6},{6,4},{8,10},{10,8},{12,14},{14,12},{16,18},{18,... | collective-permute-start | bytes 12976136 | tf_op jit(solution)/shard_map/ppermute | solution.py:560
  160.2 2.2 copy-start
  167.4 18.9 %collective-permute-start.1 = (bf16[4,24,1408]{2,1,0:T(8,128)(2,1)S(1)}, bf16[4,24,1408]{2,1,0:T(8,128)(2,1)S(1)}, u32[]{:S(2)}, u32[]{:S(2)}) collective-permute-start(bf16[4,24,1408]{2,1,0:T(8,128)(2,1)S(1)} %get-tuple-element.78), channel_id=1, source_target_pairs={{0,16},{2,18},{4,20},{6,22},{8,24},{10,26},{12,28},{14,30},{16,32}... | collective-permute-start | bytes 811016 | tf_op jit(solution)/shard_map/ppermute | solution.py:493
  169.0 17.3 %collective-permute-start.2 = (bf16[4,24,1408]{2,1,0:T(8,128)(2,1)S(1)}, bf16[4,24,1408]{2,1,0:T(8,128)(2,1)S(1)}, u32[]{:S(2)}, u32[]{:S(2)}) collective-permute-start(bf16[4,24,1408]{2,1,0:T(8,128)(2,1)S(1)} %get-tuple-element.79), channel_id=1, source_target_pairs={{0,48},{2,50},{4,52},{6,54},{8,56},{10,58},{12,60},{14,62},{16,0},... | collective-permute-start | bytes 811016 | tf_op jit(solution)/shard_map/ppermute | solution.py:493
  170.7 16.0 %collective-permute-start.3 = (bf16[4,24,1408]{2,1,0:T(8,128)(2,1)S(1)}, bf16[4,24,1408]{2,1,0:T(8,128)(2,1)S(1)}, u32[]{:S(2)}, u32[]{:S(2)}) collective-permute-start(bf16[4,24,1408]{2,1,0:T(8,128)(2,1)S(1)} %get-tuple-element.82), channel_id=1, source_target_pairs={{0,4},{2,6},{4,8},{6,10},{8,12},{10,14},{12,0},{14,2},{16,20},{18,... | collective-permute-start | bytes 811016 | tf_op jit(solution)/shard_map/ppermute | solution.py:493
  172.3 14.4 %collective-permute-start.4 = (bf16[4,24,1408]{2,1,0:T(8,128)(2,1)S(1)}, bf16[4,24,1408]{2,1,0:T(8,128)(2,1)S(1)}, u32[]{:S(2)}, u32[]{:S(2)}) collective-permute-start(bf16[4,24,1408]{2,1,0:T(8,128)(2,1)S(1)} %get-tuple-element.83), channel_id=1, source_target_pairs={{0,12},{2,14},{4,0},{6,2},{8,4},{10,6},{12,8},{14,10},{16,28},{18,... | collective-permute-start | bytes 811016 | tf_op jit(solution)/shard_map/ppermute | solution.py:493
  187.0 15.3 %collective-permute-start.5 = (bf16[2,4,24,1408]{3,2,1,0:T(8,128)(2,1)S(1)}, bf16[2,4,24,1408]{3,2,1,0:T(8,128)(2,1)S(1)}, u32[]{:S(2)}, u32[]{:S(2)}) collective-permute-start(bf16[2,4,24,1408]{3,2,1,0:T(8,128)(2,1)S(1)} %get-tuple-element.84), channel_id=1, source_target_pairs={{0,16},{2,18},{4,20},{6,22},{8,24},{10,26},{12,28},{14,30},{16,32}... | collective-permute-start | bytes 1622024 | tf_op jit(solution)/shard_map/ppermute | solution.py:495
  188.5 14.0 %collective-permute-start.6 = (bf16[2,4,24,1408]{3,2,1,0:T(8,128)(2,1)S(1)}, bf16[2,4,24,1408]{3,2,1,0:T(8,128)(2,1)S(1)}, u32[]{:S(2)}, u32[]{:S(2)}) collective-permute-start(bf16[2,4,24,1408]{3,2,1,0:T(8,128)(2,1)S(1)} %get-tuple-element.85), channel_id=1, source_target_pairs={{0,48},{2,50},{4,52},{6,54},{8,56},{10,58},{12,60},{14,62},{16,0},... | collective-permute-start | bytes 1622024 | tf_op jit(solution)/shard_map/ppermute | solution.py:495
  190.3 14.7 %collective-permute-start.7 = (bf16[2,4,24,1408]{3,2,1,0:T(8,128)(2,1)S(1)}, bf16[2,4,24,1408]{3,2,1,0:T(8,128)(2,1)S(1)}, u32[]{:S(2)}, u32[]{:S(2)}) collective-permute-start(bf16[2,4,24,1408]{3,2,1,0:T(8,128)(2,1)S(1)} %get-tuple-element.87), channel_id=1, source_target_pairs={{0,4},{2,6},{4,8},{6,10},{8,12},{10,14},{12,0},{14,2},{16,20},{18,... | collective-permute-start | bytes 1622024 | tf_op jit(solution)/shard_map/ppermute | solution.py:495
  193.4 13.4 %collective-permute-start.8 = (bf16[2,4,24,1408]{3,2,1,0:T(8,128)(2,1)S(1)}, bf16[2,4,24,1408]{3,2,1,0:T(8,128)(2,1)S(1)}, u32[]{:S(2)}, u32[]{:S(2)}) collective-permute-start(bf16[2,4,24,1408]{3,2,1,0:T(8,128)(2,1)S(1)} %get-tuple-element.88), channel_id=1, source_target_pairs={{0,12},{2,14},{4,0},{6,2},{8,4},{10,6},{12,8},{14,10},{16,28},{18,... | collective-permute-start | bytes 1622024 | tf_op jit(solution)/shard_map/ppermute | solution.py:495
  208.7 7.9 %collective-permute-start.9 = (bf16[2,24,1408]{2,1,0:T(8,128)(2,1)S(1)}, bf16[2,24,1408]{2,1,0:T(8,128)(2,1)S(1)}, u32[]{:S(2)}, u32[]{:S(2)}) collective-permute-start(bf16[2,24,1408]{2,1,0:T(8,128)(2,1)S(1)} %get-tuple-element.90), channel_id=1, source_target_pairs={{0,4},{2,6},{4,8},{6,10},{8,12},{10,14},{12,0},{14,2},{16,20},{18,... | collective-permute-start | bytes 405512 | tf_op jit(solution)/shard_map/ppermute | solution.py:497
  209.1 7.6 %collective-permute-start.10 = (bf16[2,24,1408]{2,1,0:T(8,128)(2,1)S(1)}, bf16[2,24,1408]{2,1,0:T(8,128)(2,1)S(1)}, u32[]{:S(2)}, u32[]{:S(2)}) collective-permute-start(bf16[2,24,1408]{2,1,0:T(8,128)(2,1)S(1)} %get-tuple-element.91), channel_id=1, source_target_pairs={{0,8},{2,10},{4,12},{6,14},{8,0},{10,2},{12,4},{14,6},{16,24},{18,... | collective-permute-start | bytes 405512 | tf_op jit(solution)/shard_map/ppermute | solution.py:497
  211.8 5.6 %collective-permute-start.11 = (bf16[2,24,1408]{2,1,0:T(8,128)(2,1)S(1)}, bf16[2,24,1408]{2,1,0:T(8,128)(2,1)S(1)}, u32[]{:S(2)}, u32[]{:S(2)}) collective-permute-start(bf16[2,24,1408]{2,1,0:T(8,128)(2,1)S(1)} %get-tuple-element.92), channel_id=1, source_target_pairs={{0,12},{2,14},{4,0},{6,2},{8,4},{10,6},{12,8},{14,10},{16,28},{18,... | collective-permute-start | bytes 405512 | tf_op jit(solution)/shard_map/ppermute | solution.py:497
  212.1 7.7 %collective-permute-start.12 = (bf16[2,24,1408]{2,1,0:T(8,128)(2,1)S(1)}, bf16[2,24,1408]{2,1,0:T(8,128)(2,1)S(1)}, u32[]{:S(2)}, u32[]{:S(2)}) collective-permute-start(bf16[2,24,1408]{2,1,0:T(8,128)(2,1)S(1)} %get-tuple-element.94), channel_id=1, source_target_pairs={{0,16},{2,18},{4,20},{6,22},{8,24},{10,26},{12,28},{14,30},{16,32}... | collective-permute-start | bytes 405512 | tf_op jit(solution)/shard_map/ppermute | solution.py:498
  212.1 7.7 %collective-permute-start.13 = (bf16[2,24,1408]{2,1,0:T(8,128)(2,1)S(1)}, bf16[2,24,1408]{2,1,0:T(8,128)(2,1)S(1)}, u32[]{:S(2)}, u32[]{:S(2)}) collective-permute-start(bf16[2,24,1408]{2,1,0:T(8,128)(2,1)S(1)} %get-tuple-element.95), channel_id=1, source_target_pairs={{0,32},{2,34},{4,36},{6,38},{8,40},{10,42},{12,44},{14,46},{16,48}... | collective-permute-start | bytes 405512 | tf_op jit(solution)/shard_map/ppermute | solution.py:498
  216.7 5.0 %collective-permute-start.14 = (bf16[2,24,1408]{2,1,0:T(8,128)(2,1)S(1)}, bf16[2,24,1408]{2,1,0:T(8,128)(2,1)S(1)}, u32[]{:S(2)}, u32[]{:S(2)}) collective-permute-start(bf16[2,24,1408]{2,1,0:T(8,128)(2,1)S(1)} %get-tuple-element.96), channel_id=1, source_target_pairs={{0,48},{2,50},{4,52},{6,54},{8,56},{10,58},{12,60},{14,62},{16,0},... | collective-permute-start | bytes 405512 | tf_op jit(solution)/shard_map/ppermute | solution.py:498
  223.0 5.2 %collective-permute-start.15 = (bf16[2,24,1408]{2,1,0:T(8,128)(2,1)}, bf16[2,24,1408]{2,1,0:T(8,128)(2,1)S(1)}, u32[]{:S(2)}, u32[]{:S(2)}) collective-permute-start(bf16[2,24,1408]{2,1,0:T(8,128)(2,1)} %get-tuple-element.98), channel_id=1, source_target_pairs={{0,64},{2,66},{4,68},{6,70},{8,72},{10,74},{12,76},{14,78},{16,80}... | collective-permute-start | bytes 405512 | tf_op jit(solution)/shard_map/ppermute | solution.py:500

commit v4 on v3

--- a/solution.py
+++ b/solution.py
@@ -165,7 +165,7 @@
         gout = grad_ref[h]
         scores = mm(key.T, query) * scale
         expo = jnp.exp(scores - jnp.max(scores, axis=0, keepdims=True))
-        prob = expo / jnp.sum(expo, axis=0, keepdims=True)
+        prob = expo * (1.0 / jnp.sum(expo, axis=0, keepdims=True))
         weights = prob.astype(BF)
         attn_ref[h * HEAD_DIM : (h + 1) * HEAD_DIM, :] = mm(value, weights)
         dvalue = mm(gout, weights, NT)

time: 234 us -> 234 us (level)
  no operation moved by 1% of the time
where the time goes in v4:
time: 234 us; the launch traced here: 230 us
  Pallas kernels  115 us (49%)
  waiting for transfers between devices  61.4 us (26%)
  starting transfers between devices  46.7 us (20%)
  local copies, waits for them, and re-layouts  5.43 us (2%)
    pallas_call x2, Pallas kernels, attend(): pl.pallas_call(attend_kernel, grid=(2,), in_specs=[pl.BlockSpec(memory_sp...  41.8 us
    pallas_call x4, Pallas kernels, weight_grads(): pl.pallas_call(weights_kernel, grid_spec=pltpu.PrefetchScalarGridSpec(num...  31.3 us
    all_to_all x2, waiting for transfers between devices, to_patches(): lax.all_to_all(rows.reshape(n_seq, 16, width), 'seq', split_axis=0, conca...  26.4 us
    all_to_all x2, starting transfers between devices, to_patches(): lax.all_to_all(rows.reshape(n_seq, 16, width), 'seq', split_axis=0, conca...  17.8 us
    ppermute x4, waiting for transfers between devices, sum_over_chips(): lax.ppermute(value, 'seq', to(*step))  13.2 us
    ppermute x4, waiting for transfers between devices, sum_over_chips(): lax.ppermute(first[n], 'seq', to(*step))  12.7 us
    pallas_call x1, Pallas kernels, input_grads(): pl.pallas_call(input_kernel, in_specs=[hbm, hbm, hbm], out_specs=hbm, out...  12.6 us
    pallas_call x2, Pallas kernels, pack(): pl.pallas_call(pack_kernel, grid=(2,), in_specs=[spec, spec], out_specs=p...  9.7 us
  transfers between devices with their start and end apart: 19, of which 13 were waited for; matrix products, arithmetic and copies ran while one was open for 0% of the time, Pallas kernels for 33%

profile of v4, /device:TPU:32, one launch (start us, length us, event | category | flops | bytes accessed | tf_op | source)
XLA Modules:
  0.0 229.5 jit_solution(13405531996821634043)
XLA Ops:
  0.6 4.9 %pack_rows.2 = bf16[1024,1408]{1,0:T(8,128)(2,1)} custom-call(bf16[4,256,1408]{2,1,0:T(8,128)(2,1)} %bitcast.30, bf16[4,256,1408]{2,1,0:T(8,128)(2,1)} %bitcast.32), custom_call_target="tpu_custom_call" | custom-call | flops 1000000 | bytes 1000000 | tf_op jit(solution)/shard_map/pack_rows/pallas_call | solution.py:59
  5.5 9.0 %all-to-all-start = ((bf16[64,16,1408]{2,1,0:T(8,128)(2,1)}), bf16[64,16,1408]{2,1,0:T(8,128)(2,1)S(1)}, u32[]{:S(2)}, u32[]{:S(2)}) async-start(bf16[64,16,1408]{2,1,0:T(8,128)(2,1)} %bitcast.34), calls=%async_computation | async-start | bytes 5767168 | tf_op jit(solution)/shard_map/all_to_all | solution.py:539
  14.6 4.8 %pack_rows.3 = bf16[1024,1408]{1,0:T(8,128)(2,1)} custom-call(bf16[4,256,1408]{2,1,0:T(8,128)(2,1)} %bitcast.31, bf16[4,256,1408]{2,1,0:T(8,128)(2,1)} %bitcast.33), custom_call_target="tpu_custom_call" | custom-call | flops 1000000 | bytes 1000000 | tf_op jit(solution)/shard_map/pack_rows/pallas_call | solution.py:59
  19.4 6.9 %turn_weights.1.w_any = bf16[2,2112,704]{2,1,0:T(8,128)(2,1)} custom-call(bf16[2112,1408]{1,0:T(8,128)(2,1)} %bitcast.24), custom_call_target="tpu_custom_call" | custom-call | flops 1000000 | bytes 1000000 | tf_op jit(solution)/shard_map/turn_weights/pallas_call | solution.py:80
  26.2 25.4 %all-to-all-done = bf16[64,16,1408]{2,1,0:T(8,128)(2,1)S(1)} async-done(((bf16[64,16,1408]{2,1,0:T(8,128)(2,1)}), bf16[64,16,1408]{2,1,0:T(8,128)(2,1)S(1)}, u32[]{:S(2)}, u32[]{:S(2)}) %all-to-all-start) | async-done | bytes 2883616 | tf_op jit(solution)/shard_map/all_to_all | solution.py:539
  51.6 0.0 copy-start.2
  51.7 1.6 copy-done.2
  53.3 8.7 %all-to-all-start.1 = ((bf16[64,16,1408]{2,1,0:T(8,128)(2,1)}), bf16[64,16,1408]{2,1,0:T(8,128)(2,1)S(1)}, u32[]{:S(2)}, u32[]{:S(2)}) async-start(bf16[64,16,1408]{2,1,0:T(8,128)(2,1)} %bitcast.6), calls=%async_computation.1 | async-start | bytes 5767168 | tf_op jit(solution)/shard_map/all_to_all | solution.py:539
  62.1 0.1 pad_add_fusion.at_ref
  62.2 20.8 %attend.2 = (bf16[2,768,512]{2,1,0:T(8,128)(2,1)}, bf16[2,768,512]{2,1,0:T(8,128)(2,1)}, bf16[2,768,512]{2,1,0:T(8,128)(2,1)}, bf16[2,256,2176]{2,1,0:T(8,128)(2,1)}, bf16[2,256,1408]{2,1,0:T(8,128)(2,1)}) custom-call(bf16[1024,1408]{1,0:T(8,128)(2,1)} %bitcast.36, bf16[2112,1408]{1,0:T(8,128)(2,1)} %bitcast.25, bf16[704,1408]{1,0:T(8,128)(2,1)} %wo_any.3), custom_call_target="tpu_custom_call" | custom-call | flops 1000000 | bytes 1000000 | tf_op jit(solution)/shard_map/attend/pallas_call | solution.py:195
  83.0 7.5 %weight_grads.5.refs_0_ = bf16[32,24,2816]{2,1,0:T(8,128)(2,1)} custom-call(s32[1]{0:T(128)} %bitcast.8.core_ref, bf16[2,768,512]{2,1,0:T(8,128)(2,1)} %get-tuple-element.54.xt_ref, bf16[2,768,512]{2,1,0:T(8,128)(2,1)} %get-tuple-element.55.low_ref, bf16[2,768,512]{2,1,0:T(8,128)(2,1)} %get-tuple-element.56.high_ref, bf16[512,2176]{1,0:T(8,128)(2,1)} %bitcast.27, ...), custom_call_target="tpu_custom_call" | custom-call | flops 1000000 | bytes 1000000 | tf_op jit(solution)/shard_map/weight_grads/pallas_call | solution.py:316
  90.5 7.5 %weight_grads.4.refs_0_ = bf16[32,24,2816]{2,1,0:T(8,128)(2,1)} custom-call(s32[1]{0:T(128)S(6)} %sub.14.core_ref, bf16[2,768,512]{2,1,0:T(8,128)(2,1)} %get-tuple-element.54.xt_ref, bf16[2,768,512]{2,1,0:T(8,128)(2,1)} %get-tuple-element.55.low_ref, bf16[2,768,512]{2,1,0:T(8,128)(2,1)} %get-tuple-element.56.high_ref, bf16[512,2176]{1,0:T(8,128)(2,1)} %bitcast.28, ...), custom_call_target="tpu_custom_call" | custom-call | flops 1000000 | bytes 1000000 | tf_op jit(solution)/shard_map/weight_grads/pallas_call | solution.py:316
  98.0 1.0 all-to-all-done.1
  99.1 0.0 copy-start.1
  99.1 1.6 copy-done.1
  100.6 21.0 %attend.3 = (bf16[2,768,512]{2,1,0:T(8,128)(2,1)}, bf16[2,768,512]{2,1,0:T(8,128)(2,1)}, bf16[2,768,512]{2,1,0:T(8,128)(2,1)}, bf16[2,256,2176]{2,1,0:T(8,128)(2,1)}, bf16[2,256,1408]{2,1,0:T(8,128)(2,1)}) custom-call(bf16[1024,1408]{1,0:T(8,128)(2,1)} %bitcast.35, bf16[2112,1408]{1,0:T(8,128)(2,1)} %bitcast.26, bf16[704,1408]{1,0:T(8,128)(2,1)} %wo_any.3), custom_call_target="tpu_custom_call" | custom-call | flops 1000000 | bytes 1000000 | tf_op jit(solution)/shard_map/attend/pallas_call | solution.py:195
  121.6 12.6 %input_grads.1 = bf16[64,2,16,704]{3,2,1,0:T(8,128)(2,1)} custom-call(bf16[2,256,2176]{2,1,0:T(8,128)(2,1)} %get-tuple-element.65.first_any, bf16[2,256,2176]{2,1,0:T(8,128)(2,1)} %get-tuple-element.71.second_any, bf16[2,2112,704]{2,1,0:T(8,128)(2,1)} %turn_weights.1.w_any), custom_call_target="tpu_custom_call" | custom-call | flops 1000000 | bytes 1000000 | tf_op jit(solution)/shard_map/input_grads/pallas_call | solution.py:273
  134.3 9.5 %all-to-all-start.2 = ((bf16[128,16,704]{2,1,0:T(8,128)(2,1)}), bf16[128,16,704]{2,1,0:T(8,128)(2,1)S(1)}, u32[]{:S(2)}, u32[]{:S(2)}) async-start(bf16[128,16,704]{2,1,0:T(8,128)(2,1)} %bitcast.29), calls=%async_computation.2 | async-start | bytes 6291456 | tf_op jit(solution)/shard_map/all_to_all | solution.py:543
  143.7 8.2 %weight_grads.7 = bf16[32,24,2816]{2,1,0:T(8,128)(2,1)} custom-call(s32[1]{0:T(128)S(6)} %sub.14.core_ref, bf16[2,768,512]{2,1,0:T(8,128)(2,1)} %get-tuple-element.68.xt_ref, bf16[2,768,512]{2,1,0:T(8,128)(2,1)} %get-tuple-element.69.low_ref, bf16[2,768,512]{2,1,0:T(8,128)(2,1)} %get-tuple-element.70.high_ref, bf16[512,2176]{1,0:T(8,128)(2,1)} %bitcast.37, ...), custom_call_target="tpu_custom_call" | custom-call | flops 1000000 | bytes 1000000 | tf_op jit(solution)/shard_map/weight_grads/pallas_call | solution.py:316
  151.9 0.1 collective-permute-start
  152.0 8.1 %weight_grads.6 = bf16[32,24,2816]{2,1,0:T(8,128)(2,1)} custom-call(s32[1]{0:T(128)} %bitcast.8.core_ref, bf16[2,768,512]{2,1,0:T(8,128)(2,1)} %get-tuple-element.68.xt_ref, bf16[2,768,512]{2,1,0:T(8,128)(2,1)} %get-tuple-element.69.low_ref, bf16[2,768,512]{2,1,0:T(8,128)(2,1)} %get-tuple-element.70.high_ref, bf16[512,2176]{1,0:T(8,128)(2,1)} %bitcast.38, ...), custom_call_target="tpu_custom_call" | custom-call | flops 99999997952 | bytes 1000000 | tf_op jit(solution)/shard_map/weight_grads/pallas_call | solution.py:316
  160.2 0.0 collective-permute-done
  160.2 0.0 copy-start
  160.2 2.2 copy-done
  162.4 5.0 %core_sum.1 = (bf16[2,4,24,1408]{3,2,1,0:T(8,128)(2,1)S(1)}, bf16[2,4,24,1408]{3,2,1,0:T(8,128)(2,1)S(1)}, bf16[2,4,24,1408]{3,2,1,0:T(8,128)(2,1)S(1)}, bf16[4,...) custom-call(s32[3]{0:T(128)S(1)} %pad_add_fusion.at_ref, ...), custom_call_target="tpu_custom_call" | custom-call | flops 1000000 | bytes 1000000 | tf_op jit(solution)/shard_map/core_sum/pallas_call | solution.py:368
  167.4 1.6 collective-permute-start.1
  169.0 1.8 collective-permute-start.2
  170.7 1.5 collective-permute-start.3
  172.3 1.7 collective-permute-start.4
  174.0 12.3 %collective-permute-done.1.refs_2_ = bf16[4,24,1408]{2,1,0:T(8,128)(2,1)S(1)} collective-permute-done((bf16[4,24,1408]{2,1,0:T(8,128)(2,1)S(1)}, bf16[4,24,1408]{2,1,0:T(8,128)(2,1)S(1)}, u32[]{:S(2)}, u32[]{:S(2)}) %collective-permute-start.1) | collective-permute-done | bytes 270368 | tf_op jit(solution)/shard_map/ppermute | solution.py:493
  186.3 0.0 collective-permute-done.2.refs_3_
  186.3 0.4 collective-permute-done.3.refs_6_
  186.7 0.0 collective-permute-done.4.refs_7_
  186.7 0.3 pass_on.1
  187.0 1.5 collective-permute-start.5
  188.5 1.8 collective-permute-start.6
  190.3 3.1 %collective-permute-start.7 = (bf16[2,4,24,1408]{3,2,1,0:T(8,128)(2,1)S(1)}, bf16[2,4,24,1408]{3,2,1,0:T(8,128)(2,1)S(1)}, u32[]{:S(2)}, u32[]{:S(2)}) collective-permute-start(bf16[2,4,24,1408]{3,2,1,0:T(8,128)(2,1)S(1)} %get-tuple-element.87), channel_id=1, source_target_pairs={{0,4},{2,6},{4,8},{6,10},{8,12},{10,14},{12,0},{14,2},{16,20},{18,... | collective-permute-start | bytes 1622024 | tf_op jit(solution)/shard_map/ppermute | solution.py:495
  193.4 0.1 collective-permute-start.8
  193.5 8.7 %collective-permute-done.5.refs_1_ = bf16[2,4,24,1408]{3,2,1,0:T(8,128)(2,1)S(1)} collective-permute-done((bf16[2,4,24,1408]{3,2,1,0:T(8,128)(2,1)S(1)}, bf16[2,4,24,1408]{3,2,1,0:T(8,128)(2,1)S(1)}, u32[]{:S(2)}, u32[]{:S(2)}) %collective-permute-start.5) | collective-permute-done | bytes 540704 | tf_op jit(solution)/shard_map/ppermute | solution.py:495
  202.3 0.2 collective-permute-done.6.refs_2_
  202.5 2.5 %collective-permute-done.7.refs_4_ = bf16[2,4,24,1408]{3,2,1,0:T(8,128)(2,1)S(1)} collective-permute-done((bf16[2,4,24,1408]{3,2,1,0:T(8,128)(2,1)S(1)}, bf16[2,4,24,1408]{3,2,1,0:T(8,128)(2,1)S(1)}, u32[]{:S(2)}, u32[]{:S(2)}) %collective-permute-start.7) | collective-permute-done | bytes 540704 | tf_op jit(solution)/shard_map/ppermute | solution.py:495
  205.0 1.7 collective-permute-done.8.refs_5_
  206.8 2.0 ring_sum.1
  208.7 0.4 collective-permute-start.9
  209.1 2.7 %collective-permute-start.10 = (bf16[2,24,1408]{2,1,0:T(8,128)(2,1)S(1)}, bf16[2,24,1408]{2,1,0:T(8,128)(2,1)S(1)}, u32[]{:S(2)}, u32[]{:S(2)}) collective-permute-start(bf16[2,24,1408]{2,1,0:T(8,128)(2,1)S(1)} %get-tuple-element.91), channel_id=1, source_target_pairs={{0,8},{2,10},{4,12},{6,14},{8,0},{10,2},{12,4},{14,6},{16,24},{18,... | collective-permute-start | bytes 405512 | tf_op jit(solution)/shard_map/ppermute | solution.py:497
  211.8 0.3 collective-permute-start.11
  212.1 0.0 collective-permute-start.12
  212.1 2.9 %collective-permute-start.13 = (bf16[2,24,1408]{2,1,0:T(8,128)(2,1)S(1)}, bf16[2,24,1408]{2,1,0:T(8,128)(2,1)S(1)}, u32[]{:S(2)}, u32[]{:S(2)}) collective-permute-start(bf16[2,24,1408]{2,1,0:T(8,128)(2,1)S(1)} %get-tuple-element.95), channel_id=1, source_target_pairs={{0,32},{2,34},{4,36},{6,38},{8,40},{10,42},{12,44},{14,46},{16,48}... | collective-permute-start | bytes 405512 | tf_op jit(solution)/shard_map/ppermute | solution.py:498
  215.0 1.7 collective-permute-done.9.refs_1_
  216.7 0.0 collective-permute-start.14
  216.7 0.0 collective-permute-done.10.refs_2_
  216.7 0.7 collective-permute-done.11.refs_3_
  217.4 2.4 %collective-permute-done.12.refs_5_ = bf16[2,24,1408]{2,1,0:T(8,128)(2,1)S(1)} collective-permute-done((bf16[2,24,1408]{2,1,0:T(8,128)(2,1)S(1)}, bf16[2,24,1408]{2,1,0:T(8,128)(2,1)S(1)}, u32[]{:S(2)}, u32[]{:S(2)}) %collective-permute-start.12) | collective-permute-done | bytes 135200 | tf_op jit(solution)/shard_map/ppermute | solution.py:498
  219.8 0.0 collective-permute-done.13.refs_6_
  219.8 1.9 collective-permute-done.14.refs_7_
  221.7 1.3 pair_sum.1
  223.0 0.0 collective-permute-start.15
  223.0 0.0 all-to-all-done.2.x_ref
  223.0 2.9 %unpack_rows.1 = bf16[704,1024]{1,0:T(8,128)(2,1)} custom-call(bf16[128,16,704]{2,1,0:T(8,128)(2,1)S(1)} %all-to-all-done.2.x_ref), custom_call_target="tpu_custom_call" | custom-call | flops 1000000 | bytes 1000000 | tf_op jit(solution)/shard_map/unpack_rows/pallas_call | solution.py:520
  226.0 2.3 %collective-permute-done.15.other_ref = bf16[2,24,1408]{2,1,0:T(8,128)(2,1)S(1)} collective-permute-done((bf16[2,24,1408]{2,1,0:T(8,128)(2,1)}, bf16[2,24,1408]{2,1,0:T(8,128)(2,1)S(1)}, u32[]{:S(2)}, u32[]{:S(2)}) %collective-permute-start.15) | collective-permute-done | bytes 135200 | tf_op jit(solution)/shard_map/ppermute | solution.py:500
  228.3 0.8 final_sum.1
Async XLA Ops:
  5.5 46.1 %all-to-all-start = ((bf16[64,16,1408]{2,1,0:T(8,128)(2,1)}), bf16[64,16,1408]{2,1,0:T(8,128)(2,1)S(1)}, u32[]{:S(2)}, u32[]{:S(2)}) async-start(bf16[64,16,1408]{2,1,0:T(8,128)(2,1)} %bitcast.34), calls=%async_computation | async-start | bytes 5767168 | tf_op jit(solution)/shard_map/all_to_all | solution.py:539
  51.6 1.6 copy-start.2
  53.3 45.8 %all-to-all-start.1 = ((bf16[64,16,1408]{2,1,0:T(8,128)(2,1)}), bf16[64,16,1408]{2,1,0:T(8,128)(2,1)S(1)}, u32[]{:S(2)}, u32[]{:S(2)}) async-start(bf16[64,16,1408]{2,1,0:T(8,128)(2,1)} %bitcast.6), calls=%async_computation.1 | async-start | bytes 5767168 | tf_op jit(solution)/shard_map/all_to_all | solution.py:539
  99.1 1.6 copy-start.1
  134.3 88.8 %all-to-all-start.2 = ((bf16[128,16,704]{2,1,0:T(8,128)(2,1)}), bf16[128,16,704]{2,1,0:T(8,128)(2,1)S(1)}, u32[]{:S(2)}, u32[]{:S(2)}) async-start(bf16[128,16,704]{2,1,0:T(8,128)(2,1)} %bitcast.29), calls=%async_computation.2 | async-start | bytes 6291456 | tf_op jit(solution)/shard_map/all_to_all | solution.py:543
  151.9 8.3 %collective-permute-start = (bf16[32,24,2816]{2,1,0:T(8,128)(2,1)}, bf16[32,24,2816]{2,1,0:T(8,128)(2,1)}, u32[]{:S(2)}, u32[]{:S(2)}) collective-permute-start(bf16[32,24,2816]{2,1,0:T(8,128)(2,1)} %weight_grads.7), channel_id=1, source_target_pairs={{0,2},{2,0},{4,6},{6,4},{8,10},{10,8},{12,14},{14,12},{16,18},{18,... | collective-permute-start | bytes 12976136 | tf_op jit(solution)/shard_map/ppermute | solution.py:560
  160.2 2.2 copy-start
  167.4 18.9 %collective-permute-start.1 = (bf16[4,24,1408]{2,1,0:T(8,128)(2,1)S(1)}, bf16[4,24,1408]{2,1,0:T(8,128)(2,1)S(1)}, u32[]{:S(2)}, u32[]{:S(2)}) collective-permute-start(bf16[4,24,1408]{2,1,0:T(8,128)(2,1)S(1)} %get-tuple-element.78), channel_id=1, source_target_pairs={{0,16},{2,18},{4,20},{6,22},{8,24},{10,26},{12,28},{14,30},{16,32}... | collective-permute-start | bytes 811016 | tf_op jit(solution)/shard_map/ppermute | solution.py:493
  169.0 17.3 %collective-permute-start.2 = (bf16[4,24,1408]{2,1,0:T(8,128)(2,1)S(1)}, bf16[4,24,1408]{2,1,0:T(8,128)(2,1)S(1)}, u32[]{:S(2)}, u32[]{:S(2)}) collective-permute-start(bf16[4,24,1408]{2,1,0:T(8,128)(2,1)S(1)} %get-tuple-element.79), channel_id=1, source_target_pairs={{0,48},{2,50},{4,52},{6,54},{8,56},{10,58},{12,60},{14,62},{16,0},... | collective-permute-start | bytes 811016 | tf_op jit(solution)/shard_map/ppermute | solution.py:493
  170.7 16.0 %collective-permute-start.3 = (bf16[4,24,1408]{2,1,0:T(8,128)(2,1)S(1)}, bf16[4,24,1408]{2,1,0:T(8,128)(2,1)S(1)}, u32[]{:S(2)}, u32[]{:S(2)}) collective-permute-start(bf16[4,24,1408]{2,1,0:T(8,128)(2,1)S(1)} %get-tuple-element.82), channel_id=1, source_target_pairs={{0,4},{2,6},{4,8},{6,10},{8,12},{10,14},{12,0},{14,2},{16,20},{18,... | collective-permute-start | bytes 811016 | tf_op jit(solution)/shard_map/ppermute | solution.py:493
  172.3 14.4 %collective-permute-start.4 = (bf16[4,24,1408]{2,1,0:T(8,128)(2,1)S(1)}, bf16[4,24,1408]{2,1,0:T(8,128)(2,1)S(1)}, u32[]{:S(2)}, u32[]{:S(2)}) collective-permute-start(bf16[4,24,1408]{2,1,0:T(8,128)(2,1)S(1)} %get-tuple-element.83), channel_id=1, source_target_pairs={{0,12},{2,14},{4,0},{6,2},{8,4},{10,6},{12,8},{14,10},{16,28},{18,... | collective-permute-start | bytes 811016 | tf_op jit(solution)/shard_map/ppermute | solution.py:493
  187.0 15.3 %collective-permute-start.5 = (bf16[2,4,24,1408]{3,2,1,0:T(8,128)(2,1)S(1)}, bf16[2,4,24,1408]{3,2,1,0:T(8,128)(2,1)S(1)}, u32[]{:S(2)}, u32[]{:S(2)}) collective-permute-start(bf16[2,4,24,1408]{3,2,1,0:T(8,128)(2,1)S(1)} %get-tuple-element.84), channel_id=1, source_target_pairs={{0,16},{2,18},{4,20},{6,22},{8,24},{10,26},{12,28},{14,30},{16,32}... | collective-permute-start | bytes 1622024 | tf_op jit(solution)/shard_map/ppermute | solution.py:495
  188.5 14.0 %collective-permute-start.6 = (bf16[2,4,24,1408]{3,2,1,0:T(8,128)(2,1)S(1)}, bf16[2,4,24,1408]{3,2,1,0:T(8,128)(2,1)S(1)}, u32[]{:S(2)}, u32[]{:S(2)}) collective-permute-start(bf16[2,4,24,1408]{3,2,1,0:T(8,128)(2,1)S(1)} %get-tuple-element.85), channel_id=1, source_target_pairs={{0,48},{2,50},{4,52},{6,54},{8,56},{10,58},{12,60},{14,62},{16,0},... | collective-permute-start | bytes 1622024 | tf_op jit(solution)/shard_map/ppermute | solution.py:495
  190.3 14.7 %collective-permute-start.7 = (bf16[2,4,24,1408]{3,2,1,0:T(8,128)(2,1)S(1)}, bf16[2,4,24,1408]{3,2,1,0:T(8,128)(2,1)S(1)}, u32[]{:S(2)}, u32[]{:S(2)}) collective-permute-start(bf16[2,4,24,1408]{3,2,1,0:T(8,128)(2,1)S(1)} %get-tuple-element.87), channel_id=1, source_target_pairs={{0,4},{2,6},{4,8},{6,10},{8,12},{10,14},{12,0},{14,2},{16,20},{18,... | collective-permute-start | bytes 1622024 | tf_op jit(solution)/shard_map/ppermute | solution.py:495
  193.4 13.4 %collective-permute-start.8 = (bf16[2,4,24,1408]{3,2,1,0:T(8,128)(2,1)S(1)}, bf16[2,4,24,1408]{3,2,1,0:T(8,128)(2,1)S(1)}, u32[]{:S(2)}, u32[]{:S(2)}) collective-permute-start(bf16[2,4,24,1408]{3,2,1,0:T(8,128)(2,1)S(1)} %get-tuple-element.88), channel_id=1, source_target_pairs={{0,12},{2,14},{4,0},{6,2},{8,4},{10,6},{12,8},{14,10},{16,28},{18,... | collective-permute-start | bytes 1622024 | tf_op jit(solution)/shard_map/ppermute | solution.py:495
  208.7 7.9 %collective-permute-start.9 = (bf16[2,24,1408]{2,1,0:T(8,128)(2,1)S(1)}, bf16[2,24,1408]{2,1,0:T(8,128)(2,1)S(1)}, u32[]{:S(2)}, u32[]{:S(2)}) collective-permute-start(bf16[2,24,1408]{2,1,0:T(8,128)(2,1)S(1)} %get-tuple-element.90), channel_id=1, source_target_pairs={{0,4},{2,6},{4,8},{6,10},{8,12},{10,14},{12,0},{14,2},{16,20},{18,... | collective-permute-start | bytes 405512 | tf_op jit(solution)/shard_map/ppermute | solution.py:497
  209.1 7.6 %collective-permute-start.10 = (bf16[2,24,1408]{2,1,0:T(8,128)(2,1)S(1)}, bf16[2,24,1408]{2,1,0:T(8,128)(2,1)S(1)}, u32[]{:S(2)}, u32[]{:S(2)}) collective-permute-start(bf16[2,24,1408]{2,1,0:T(8,128)(2,1)S(1)} %get-tuple-element.91), channel_id=1, source_target_pairs={{0,8},{2,10},{4,12},{6,14},{8,0},{10,2},{12,4},{14,6},{16,24},{18,... | collective-permute-start | bytes 405512 | tf_op jit(solution)/shard_map/ppermute | solution.py:497
  211.8 5.6 %collective-permute-start.11 = (bf16[2,24,1408]{2,1,0:T(8,128)(2,1)S(1)}, bf16[2,24,1408]{2,1,0:T(8,128)(2,1)S(1)}, u32[]{:S(2)}, u32[]{:S(2)}) collective-permute-start(bf16[2,24,1408]{2,1,0:T(8,128)(2,1)S(1)} %get-tuple-element.92), channel_id=1, source_target_pairs={{0,12},{2,14},{4,0},{6,2},{8,4},{10,6},{12,8},{14,10},{16,28},{18,... | collective-permute-start | bytes 405512 | tf_op jit(solution)/shard_map/ppermute | solution.py:497
  212.1 7.7 %collective-permute-start.12 = (bf16[2,24,1408]{2,1,0:T(8,128)(2,1)S(1)}, bf16[2,24,1408]{2,1,0:T(8,128)(2,1)S(1)}, u32[]{:S(2)}, u32[]{:S(2)}) collective-permute-start(bf16[2,24,1408]{2,1,0:T(8,128)(2,1)S(1)} %get-tuple-element.94), channel_id=1, source_target_pairs={{0,16},{2,18},{4,20},{6,22},{8,24},{10,26},{12,28},{14,30},{16,32}... | collective-permute-start | bytes 405512 | tf_op jit(solution)/shard_map/ppermute | solution.py:498
  212.1 7.7 %collective-permute-start.13 = (bf16[2,24,1408]{2,1,0:T(8,128)(2,1)S(1)}, bf16[2,24,1408]{2,1,0:T(8,128)(2,1)S(1)}, u32[]{:S(2)}, u32[]{:S(2)}) collective-permute-start(bf16[2,24,1408]{2,1,0:T(8,128)(2,1)S(1)} %get-tuple-element.95), channel_id=1, source_target_pairs={{0,32},{2,34},{4,36},{6,38},{8,40},{10,42},{12,44},{14,46},{16,48}... | collective-permute-start | bytes 405512 | tf_op jit(solution)/shard_map/ppermute | solution.py:498
  216.7 5.0 %collective-permute-start.14 = (bf16[2,24,1408]{2,1,0:T(8,128)(2,1)S(1)}, bf16[2,24,1408]{2,1,0:T(8,128)(2,1)S(1)}, u32[]{:S(2)}, u32[]{:S(2)}) collective-permute-start(bf16[2,24,1408]{2,1,0:T(8,128)(2,1)S(1)} %get-tuple-element.96), channel_id=1, source_target_pairs={{0,48},{2,50},{4,52},{6,54},{8,56},{10,58},{12,60},{14,62},{16,0},... | collective-permute-start | bytes 405512 | tf_op jit(solution)/shard_map/ppermute | solution.py:498
  223.0 5.2 %collective-permute-start.15 = (bf16[2,24,1408]{2,1,0:T(8,128)(2,1)}, bf16[2,24,1408]{2,1,0:T(8,128)(2,1)S(1)}, u32[]{:S(2)}, u32[]{:S(2)}) collective-permute-start(bf16[2,24,1408]{2,1,0:T(8,128)(2,1)} %get-tuple-element.98), channel_id=1, source_target_pairs={{0,64},{2,66},{4,68},{6,70},{8,72},{10,74},{12,76},{14,78},{16,80}... | collective-permute-start | bytes 405512 | tf_op jit(solution)/shard_map/ppermute | solution.py:500
